TPU v7x, 128 devices: a whole 4x4x4 slice. The times are simulated.
128 devices in a mesh: group: 8 (over y, core), sub: 16 (over z, x).
Axes of the slice: x: 4, y: 4, z: 4, core: 2. Of those that a mesh axis runs over, the one named last changes fastest.
Arguments:
- shared_sizes: int32 [8, 16, 2], P('group', 'sub'), may hold values from 0 to 256, as said below
- stiffness: float32 [8, 16], P('group', 'sub'), may hold values from 0.1 to 10
- load_cases: float32 [8, 16, 1024, 384], P('group', 'sub'), may hold values from -6 to 6
- schur_blocks: bfloat16 [8, 16, 1024, 1024], P('group', 'sub')
- neumann_inverse: bfloat16 [8, 16, 1024, 1024], P('group', 'sub')
- coarse_basis: bfloat16 [8, 16, 32, 1024], P('group', 'sub'), may hold values from -0.1875 to 0.1875
- coarse_dofs: int32 [8, 16, 32], P('group', 'sub'), may hold values from 0 to 2047
- coarse_inverse: float32 [2048, 2048], P('sub'), as said below
Outputs:
- solution: float32 [8, 16, 1024, 384], P('group', 'sub')
- residual: float32 [8, 16, 1024, 384], P('group', 'sub')
Inputs may be any that keep to these rules, and one draw needn't show every extreme that they name: shared_sizes[g, s, 0] equals shared_sizes[g, s - 1, 1]; the lower share of the first and the upper share of the last subdomain of a group are 0, the other shares lie in 128 to 256, and in every group some subdomain shares exactly 256 with its upper neighbour. `coarse_inverse`: symmetric.
All inputs are finite; a program needn't handle non-finite values.
Results may differ from a plain program's by a relative error of at most 0.0075.
Values sent between devices are 32-bit elements; how exact they have to be, the bound alone decides.
A program may use at most 128 MiB of HBM per device.

v0:
```python
import math

import jax
import jax.numpy as jnp
from jax import lax
from jax.sharding import PartitionSpec as P

MAXSH = 256
ITERS = 4


OMEGA = 0.6


def from_behind(block, axis, distance):
    devices = range(lax.axis_size(axis))
    route = [(i - distance, i) for i in devices if i - distance in devices]
    return lax.ppermute(block, axis, route)


def extended(x, sides, width):
    for axis, dim in sides:
        peers, length = (lax.axis_size(axis), x.shape[dim])
        up = [(i, (i + 1) % peers) for i in range(peers - 1)]
        down = [(j, i) for i, j in up]
        last = lax.slice_in_dim(x, length - width, length, axis=dim)
        leading = lax.slice_in_dim(x, 0, width, axis=dim)
        before = lax.ppermute(last, axis, up)
        after = lax.ppermute(leading, axis, down)
        x = jnp.concatenate([before, x, after], axis=dim)
    return x


def in_order(parts, dim):
    parts = jnp.moveaxis(parts, 0, dim)
    shape = parts.shape
    return parts.reshape(*shape[:dim], shape[dim] * shape[dim + 1], *shape[dim + 2 :])


def from_everyone(x, axis):
    copies = jnp.broadcast_to(x, (lax.axis_size(axis), *x.shape))
    return lax.all_to_all(copies, axis, split_axis=0, concat_axis=0, tiled=True)


def gather_directly(x, axis, dim):
    return in_order(from_everyone(x, axis), dim)


def side_by_side(arrays, axis, dim, along):
    widths = [math.prod(a.shape[along:]) for a in arrays]
    both = jnp.concatenate(
        [a.reshape(*a.shape[:along], w) for a, w in zip(arrays, widths)], axis=along
    )
    whole = gather_directly(both, axis, dim)
    parts = jnp.split(whole, [sum(widths[:k]) for k in range(1, len(widths))], axis=along)
    return tuple((b.reshape(*whole.shape[:along], *a.shape[along:]) for a, b in zip(arrays, parts)))


def of_everyone(x, axis):
    return from_everyone(x, axis).sum(axis=0)


def lift_piece(tail_rows, share_size):
    slab_width = tail_rows.shape[0]
    rolled = jnp.roll(tail_rows, share_size - slab_width, axis=0)
    inside = (jnp.arange(slab_width) < share_size)[:, None]
    return jnp.where(inside, rolled, jnp.zeros_like(rolled))


def place_piece(head_rows, share_size):
    slab_width = head_rows.shape[0]
    inside = (jnp.arange(slab_width) < share_size)[:, None]
    masked = jnp.where(inside, head_rows, jnp.zeros_like(head_rows))
    return jnp.roll(masked, slab_width - share_size, axis=0)


def assemble(vector, share_up):
    unknowns = vector.shape[0]
    tail_rows = vector[unknowns - MAXSH :]
    head_rows = vector[:MAXSH]
    lifted = lift_piece(tail_rows, share_up)
    from_lower = from_behind(lifted, "sub", 1)
    from_upper = from_behind(head_rows, "sub", -1)
    placed = place_piece(from_upper, share_up)
    return jnp.concatenate(
        [head_rows + from_lower, vector[MAXSH : unknowns - MAXSH], tail_rows + placed], axis=0
    )


def on_device(
    shared_sizes,
    stiffness,
    load_cases,
    schur_blocks,
    neumann_inverse,
    coarse_basis,
    coarse_dofs,
    coarse_inverse,
):
    share_low = shared_sizes[0, 0, 0]
    share_up = shared_sizes[0, 0, 1]
    beside_all = extended(stiffness, (("sub", 1),), 1)
    own_stiff = beside_all[0, 1]
    low_weight = own_stiff / (own_stiff + beside_all[0, 0])
    up_weight = own_stiff / (own_stiff + beside_all[0, 2])
    loads = load_cases[0, 0]
    schur = schur_blocks[0, 0]
    neumann = neumann_inverse[0, 0]
    basis = coarse_basis[0, 0]
    my_dofs = coarse_dofs[0, 0]
    unknowns, cases = loads.shape
    own_count = coarse_inverse.shape[0]
    row_index = jnp.arange(unknowns)
    weight = jnp.where(
        row_index < share_low,
        low_weight,
        jnp.where(row_index >= unknowns - share_up, up_weight, jnp.float32(1.0)),
    )[:, None]
    highest = lax.Precision.HIGHEST

    def operator_residual(solution):
        return loads - jnp.dot(
            schur, solution.astype(jnp.bfloat16), preferred_element_type=jnp.float32
        )

    solution = jnp.zeros((unknowns, cases), jnp.float32)
    for sweep in range(ITERS):
        local = operator_residual(solution)
        weighted = (weight * assemble(local, share_up)).astype(jnp.bfloat16)
        coarse_terms = jnp.dot(basis, weighted, preferred_element_type=jnp.float32)
        dof_values = my_dofs.astype(jnp.float32)
        all_terms, all_dofs = side_by_side((coarse_terms, dof_values), "sub", 0, 1)
        dof_index = all_dofs.astype(jnp.int32)
        first_row = lax.axis_index("sub") * own_count
        own_select = (dof_index[:, None] == first_row + jnp.arange(own_count)[None, :]).astype(
            jnp.float32
        )
        owned = lax.dot_general(own_select, all_terms, (((0,), (0,)), ((), ())), precision=highest)
        owned = of_everyone(owned, "group")
        columns = jnp.take(coarse_inverse, dof_index, axis=1)
        partial_vals = lax.dot_general(columns, owned, (((0,), (0,)), ((), ())), precision=highest)
        partial_vals = partial_vals.reshape(-1, coarse_terms.shape[0], cases)
        received = lax.all_to_all(partial_vals, "sub", split_axis=0, concat_axis=0, tiled=True)
        picked = jnp.sum(received, axis=0)
        picked = picked.astype(jnp.bfloat16)
        correction = jnp.dot(neumann, weighted, preferred_element_type=jnp.float32)
        correction = correction + lax.dot_general(
            basis, picked, (((0,), (0,)), ((), ())), preferred_element_type=jnp.float32
        )
        solution = solution + OMEGA * assemble(weight * correction, share_up)
    residual = assemble(operator_residual(solution), share_up)
    return (solution[None, None], residual[None, None])


def solution(mesh):
    return jax.shard_map(
        on_device,
        mesh=mesh,
        in_specs=(
            P("group", "sub", None),
            P("group", "sub"),
            P("group", "sub", None, None),
            P("group", "sub", None, None),
            P("group", "sub", None, None),
            P("group", "sub", None, None),
            P("group", "sub", None),
            P("sub", None),
        ),
        out_specs=(P("group", "sub", None, None), P("group", "sub", None, None)),
        check_vma=False,
    )
```

profile of v0, /device:TPU:0, one launch (start us, length us, event | category | flops | bytes accessed | tf_op | source)
XLA Modules:
  0.0 533.5 jit_solution(11758579052873285541)
XLA Ops:
  10.5 9.5 %collective-permute-done.3 = f32[256,384]{0,1:T(8,128)S(1)} collective-permute-done((f32[256,384]{0,1:T(8,128)S(1)}, f32[256,384]{0,1:T(8,128)S(1)}, u32[]{:S(2)}, u32[]{:S(2)}) %collective-permute-start.3) | collective-permute-done | bytes 393248 | tf_op jit(solution)/shard_map/ppermute | solution.py:18
  40.7 9.7 %all-to-all-start = ((f32[16,32,385]{2,1,0:T(8,128)}), f32[16,32,385]{2,1,0:T(8,128)S(1)}, u32[]{:S(2)}, u32[]{:S(2)}) async-start(f32[16,32,385]{2,1,0:T(8,128)} %broadcast_in_dim.143), calls=%async_computation | async-start | bytes 2097152 | tf_op jit(solution)/shard_map/all_to_all | solution.py:42
  50.9 15.6 %all-to-all-done = f32[16,32,385]{2,1,0:T(8,128)S(1)} async-done(((f32[16,32,385]{2,1,0:T(8,128)}), f32[16,32,385]{2,1,0:T(8,128)S(1)}, u32[]{:S(2)}, u32[]{:S(2)}) %all-to-all-start) | async-done | bytes 788512 | tf_op jit(solution)/shard_map/all_to_all | solution.py:42
  81.1 14.6 %all-to-all-done.1 = f32[8,128,384]{2,1,0:T(8,128)} async-done(((f32[8,128,384]{2,1,0:T(8,128)}), f32[8,128,384]{2,1,0:T(8,128)}, u32[]{:S(2)}, u32[]{:S(2)}) %all-to-all-start.1) | async-done | bytes 1572896 | tf_op jit(solution)/shard_map/all_to_all | solution.py:42
  99.7 17.7 %all_to_all.60 = f32[16,32,384]{2,1,0:T(8,128)} all-to-all(f32[16,32,384]{2,1,0:T(8,128)S(1)} %fusion.113), channel_id=1, replica_groups=mesh['group'=8,'sub'=16] {'sub'}, dimensions={0} | all-to-all | bytes 1572864 | tf_op jit(solution)/shard_map/all_to_all | solution.py:143
  124.6 10.4 %collective-permute-done.5 = f32[256,384]{0,1:T(8,128)S(1)} collective-permute-done((f32[256,384]{0,1:T(8,128)S(1)}, f32[256,384]{0,1:T(8,128)S(1)}, u32[]{:S(2)}, u32[]{:S(2)}) %collective-permute-start.5) | collective-permute-done | bytes 393248 | tf_op jit(solution)/shard_map/ppermute | solution.py:18
  138.9 5.3 collective-permute-done.4
  146.9 9.3 %collective-permute-done.7 = f32[256,384]{0,1:T(8,128)S(1)} collective-permute-done((f32[256,384]{0,1:T(8,128)S(1)}, f32[256,384]{0,1:T(8,128)S(1)}, u32[]{:S(2)}, u32[]{:S(2)}) %collective-permute-start.7) | collective-permute-done | bytes 393248 | tf_op jit(solution)/shard_map/ppermute | solution.py:18
  166.6 21.5 %all_to_all.61 = f32[16,32,385]{2,1,0:T(8,128)S(1)} all-to-all(f32[16,32,385]{2,1,0:T(8,128)S(1)} %broadcast_in_dim.145), channel_id=1, replica_groups=mesh['group'=8,'sub'=16] {'sub'}, dimensions={0} | all-to-all | bytes 1576960 | tf_op jit(solution)/shard_map/all_to_all | solution.py:42
  200.6 15.9 %all-to-all-done.4 = f32[8,128,384]{2,1,0:T(8,128)} async-done(((f32[8,128,384]{2,1,0:T(8,128)}), f32[8,128,384]{2,1,0:T(8,128)}, u32[]{:S(2)}, u32[]{:S(2)}) %all-to-all-start.4) | async-done | bytes 1572896 | tf_op jit(solution)/shard_map/all_to_all | solution.py:42
  220.5 17.7 %all_to_all.62 = f32[16,32,384]{2,1,0:T(8,128)} all-to-all(f32[16,32,384]{2,1,0:T(8,128)S(1)} %fusion.111), channel_id=1, replica_groups=mesh['group'=8,'sub'=16] {'sub'}, dimensions={0} | all-to-all | bytes 1572864 | tf_op jit(solution)/shard_map/all_to_all | solution.py:143
  245.4 10.4 %collective-permute-done.9 = f32[256,384]{0,1:T(8,128)S(1)} collective-permute-done((f32[256,384]{0,1:T(8,128)S(1)}, f32[256,384]{0,1:T(8,128)S(1)}, u32[]{:S(2)}, u32[]{:S(2)}) %collective-permute-start.9) | collective-permute-done | bytes 393248 | tf_op jit(solution)/shard_map/ppermute | solution.py:18
  267.7 9.3 %collective-permute-done.11 = f32[256,384]{0,1:T(8,128)S(1)} collective-permute-done((f32[256,384]{0,1:T(8,128)S(1)}, f32[256,384]{0,1:T(8,128)S(1)}, u32[]{:S(2)}, u32[]{:S(2)}) %collective-permute-start.11) | collective-permute-done | bytes 393248 | tf_op jit(solution)/shard_map/ppermute | solution.py:18
  287.4 21.5 %all_to_all.63 = f32[16,32,385]{2,1,0:T(8,128)S(1)} all-to-all(f32[16,32,385]{2,1,0:T(8,128)S(1)} %broadcast_in_dim.147), channel_id=1, replica_groups=mesh['group'=8,'sub'=16] {'sub'}, dimensions={0} | all-to-all | bytes 1576960 | tf_op jit(solution)/shard_map/all_to_all | solution.py:42
  321.4 16.0 %all-to-all-done.7 = f32[8,128,384]{2,1,0:T(8,128)} async-done(((f32[8,128,384]{2,1,0:T(8,128)}), f32[8,128,384]{2,1,0:T(8,128)}, u32[]{:S(2)}, u32[]{:S(2)}) %all-to-all-start.7) | async-done | bytes 1572896 | tf_op jit(solution)/shard_map/all_to_all | solution.py:42
  341.4 17.7 %all_to_all.64 = f32[16,32,384]{2,1,0:T(8,128)} all-to-all(f32[16,32,384]{2,1,0:T(8,128)S(1)} %fusion.109), channel_id=1, replica_groups=mesh['group'=8,'sub'=16] {'sub'}, dimensions={0} | all-to-all | bytes 1572864 | tf_op jit(solution)/shard_map/all_to_all | solution.py:143
  366.3 10.4 %collective-permute-done.13 = f32[256,384]{0,1:T(8,128)S(1)} collective-permute-done((f32[256,384]{0,1:T(8,128)S(1)}, f32[256,384]{0,1:T(8,128)S(1)}, u32[]{:S(2)}, u32[]{:S(2)}) %collective-permute-start.13) | collective-permute-done | bytes 393248 | tf_op jit(solution)/shard_map/ppermute | solution.py:18
  389.0 9.1 %collective-permute-done.15 = f32[256,384]{0,1:T(8,128)S(1)} collective-permute-done((f32[256,384]{0,1:T(8,128)S(1)}, f32[256,384]{0,1:T(8,128)S(1)}, u32[]{:S(2)}, u32[]{:S(2)}) %collective-permute-start.15) | collective-permute-done | bytes 393248 | tf_op jit(solution)/shard_map/ppermute | solution.py:18
  408.4 21.5 %all_to_all.65 = f32[16,32,385]{2,1,0:T(8,128)S(1)} all-to-all(f32[16,32,385]{2,1,0:T(8,128)S(1)} %broadcast_in_dim.149), channel_id=1, replica_groups=mesh['group'=8,'sub'=16] {'sub'}, dimensions={0} | all-to-all | bytes 1576960 | tf_op jit(solution)/shard_map/all_to_all | solution.py:42
  439.7 18.1 %all-to-all-done.10 = f32[8,128,384]{2,1,0:T(8,128)} async-done(((f32[8,128,384]{2,1,0:T(8,128)}), f32[8,128,384]{2,1,0:T(8,128)}, u32[]{:S(2)}, u32[]{:S(2)}) %all-to-all-start.10) | async-done | bytes 1572896 | tf_op jit(solution)/shard_map/all_to_all | solution.py:42
  461.1 17.7 %all_to_all.66 = f32[16,32,384]{2,1,0:T(8,128)} all-to-all(f32[16,32,384]{2,1,0:T(8,128)S(1)} %fusion.107), channel_id=1, replica_groups=mesh['group'=8,'sub'=16] {'sub'}, dimensions={0} | all-to-all | bytes 1572864 | tf_op jit(solution)/shard_map/all_to_all | solution.py:143
  485.2 10.4 %collective-permute-done.17 = f32[256,384]{0,1:T(8,128)S(1)} collective-permute-done((f32[256,384]{0,1:T(8,128)S(1)}, f32[256,384]{0,1:T(8,128)S(1)}, u32[]{:S(2)}, u32[]{:S(2)}) %collective-permute-start.17) | collective-permute-done | bytes 393248 | tf_op jit(solution)/shard_map/ppermute | solution.py:18
  498.7 6.2 %collective-permute-done.16 = f32[256,384]{0,1:T(8,128)S(1)} collective-permute-done((f32[256,384]{0,1:T(8,128)S(1)}, f32[256,384]{0,1:T(8,128)S(1)}, u32[]{:S(2)}, u32[]{:S(2)}) %collective-permute-start.16) | collective-permute-done | bytes 393248 | tf_op jit(solution)/shard_map/ppermute | solution.py:18
  507.9 9.3 %collective-permute-done.19 = f32[256,384]{0,1:T(8,128)S(1)} collective-permute-done((f32[256,384]{0,1:T(8,128)S(1)}, f32[256,384]{0,1:T(8,128)S(1)}, u32[]{:S(2)}, u32[]{:S(2)}) %collective-permute-start.19) | collective-permute-done | bytes 393248 | tf_op jit(solution)/shard_map/ppermute | solution.py:18
  (311 shorter events, 202.4 us)
Async XLA Ops:
  7.5 12.6 %collective-permute-start.3 = (f32[256,384]{0,1:T(8,128)S(1)}, f32[256,384]{0,1:T(8,128)S(1)}, u32[]{:S(2)}, u32[]{:S(2)}) collective-permute-start(f32[256,384]{0,1:T(8,128)S(1)} %get-tuple-element.55), channel_id=1, source_target_pairs={{1,0},{2,1},{3,2},{4,3},{5,4},{6,5},{7,6},{8,7},{9,8},{10,9},{11,1... | collective-permute-start | bytes 1179656 | tf_op jit(solution)/shard_map/ppermute | solution.py:18
  21.2 15.3 %collective-permute-start.2 = (f32[256,384]{0,1:T(8,128)}, f32[256,384]{0,1:T(8,128)S(1)}, u32[]{:S(2)}, u32[]{:S(2)}) collective-permute-start(f32[256,384]{0,1:T(8,128)} %get-tuple-element.74), channel_id=1, source_target_pairs={{0,1},{1,2},{2,3},{3,4},{4,5},{5,6},{6,7},{7,8},{8,9},{9,10},{10,1... | collective-permute-start | bytes 1179656 | tf_op jit(solution)/shard_map/ppermute | solution.py:18
  24.8 9.6 %collective-permute-start.1 = (f32[1,1]{1,0:T(1,128)}, f32[1,1]{1,0:T(1,128)}, u32[]{:S(2)}, u32[]{:S(2)}) collective-permute-start(f32[1,1]{1,0:T(1,128)} %param.13), channel_id=1, source_target_pairs={{1,0},{2,1},{3,2},{4,3},{5,4},{6,5},{7,6},{8,7},{9,8},{10,9},{11,1... | collective-permute-start | bytes 20 | tf_op jit(solution)/shard_map/ppermute | solution.py:29
  26.1 9.0 %collective-permute-start = (f32[1,1]{1,0:T(1,128)}, f32[1,1]{1,0:T(1,128)}, u32[]{:S(2)}, u32[]{:S(2)}) collective-permute-start(f32[1,1]{1,0:T(1,128)} %param.13), channel_id=1, source_target_pairs={{0,1},{1,2},{2,3},{3,4},{4,5},{5,6},{6,7},{7,8},{8,9},{9,10},{10,1... | collective-permute-start | bytes 20 | tf_op jit(solution)/shard_map/ppermute | solution.py:28
  40.7 25.8 %all-to-all-start = ((f32[16,32,385]{2,1,0:T(8,128)}), f32[16,32,385]{2,1,0:T(8,128)S(1)}, u32[]{:S(2)}, u32[]{:S(2)}) async-start(f32[16,32,385]{2,1,0:T(8,128)} %broadcast_in_dim.143), calls=%async_computation | async-start | bytes 2097152 | tf_op jit(solution)/shard_map/all_to_all | solution.py:42
  69.5 26.2 %all-to-all-start.1 = ((f32[8,128,384]{2,1,0:T(8,128)}), f32[8,128,384]{2,1,0:T(8,128)}, u32[]{:S(2)}, u32[]{:S(2)}) async-start(f32[8,128,384]{2,1,0:T(8,128)} %broadcast_in_dim.144), calls=%async_computation.1 | async-start | bytes 3145728 | tf_op jit(solution)/shard_map/all_to_all | solution.py:42
  123.3 11.7 %collective-permute-start.5 = (f32[256,384]{0,1:T(8,128)S(1)}, f32[256,384]{0,1:T(8,128)S(1)}, u32[]{:S(2)}, u32[]{:S(2)}) collective-permute-start(f32[256,384]{0,1:T(8,128)S(1)} %get-tuple-element.51), channel_id=1, source_target_pairs={{1,0},{2,1},{3,2},{4,3},{5,4},{6,5},{7,6},{8,7},{9,8},{10,9},{11,1... | collective-permute-start | bytes 1179656 | tf_op jit(solution)/shard_map/ppermute | solution.py:18
  135.3 8.9 %collective-permute-start.4 = (f32[256,384]{0,1:T(8,128)S(1)}, f32[256,384]{0,1:T(8,128)S(1)}, u32[]{:S(2)}, u32[]{:S(2)}) collective-permute-start(f32[256,384]{0,1:T(8,128)S(1)} %get-tuple-element.70), channel_id=1, source_target_pairs={{0,1},{1,2},{2,3},{3,4},{4,5},{5,6},{6,7},{7,8},{8,9},{9,10},{10,1... | collective-permute-start | bytes 1179656 | tf_op jit(solution)/shard_map/ppermute | solution.py:18
  145.6 10.6 %collective-permute-start.7 = (f32[256,384]{0,1:T(8,128)S(1)}, f32[256,384]{0,1:T(8,128)S(1)}, u32[]{:S(2)}, u32[]{:S(2)}) collective-permute-start(f32[256,384]{0,1:T(8,128)S(1)} %get-tuple-element.45), channel_id=1, source_target_pairs={{1,0},{2,1},{3,2},{4,3},{5,4},{6,5},{7,6},{8,7},{9,8},{10,9},{11,1... | collective-permute-start | bytes 1179656 | tf_op jit(solution)/shard_map/ppermute | solution.py:18
  156.5 8.9 %collective-permute-start.6 = (f32[256,384]{0,1:T(8,128)S(1)}, f32[256,384]{0,1:T(8,128)S(1)}, u32[]{:S(2)}, u32[]{:S(2)}) collective-permute-start(f32[256,384]{0,1:T(8,128)S(1)} %get-tuple-element.68), channel_id=1, source_target_pairs={{0,1},{1,2},{2,3},{3,4},{4,5},{5,6},{6,7},{7,8},{8,9},{9,10},{10,1... | collective-permute-start | bytes 1179656 | tf_op jit(solution)/shard_map/ppermute | solution.py:18
  190.6 25.9 %all-to-all-start.4 = ((f32[8,128,384]{2,1,0:T(8,128)}), f32[8,128,384]{2,1,0:T(8,128)}, u32[]{:S(2)}, u32[]{:S(2)}) async-start(f32[8,128,384]{2,1,0:T(8,128)} %broadcast_in_dim.146), calls=%async_computation.4 | async-start | bytes 3145728 | tf_op jit(solution)/shard_map/all_to_all | solution.py:42
  244.1 11.7 %collective-permute-start.9 = (f32[256,384]{0,1:T(8,128)S(1)}, f32[256,384]{0,1:T(8,128)S(1)}, u32[]{:S(2)}, u32[]{:S(2)}) collective-permute-start(f32[256,384]{0,1:T(8,128)S(1)} %get-tuple-element.41), channel_id=1, source_target_pairs={{1,0},{2,1},{3,2},{4,3},{5,4},{6,5},{7,6},{8,7},{9,8},{10,9},{11,1... | collective-permute-start | bytes 1179656 | tf_op jit(solution)/shard_map/ppermute | solution.py:18
  256.1 8.9 %collective-permute-start.8 = (f32[256,384]{0,1:T(8,128)S(1)}, f32[256,384]{0,1:T(8,128)S(1)}, u32[]{:S(2)}, u32[]{:S(2)}) collective-permute-start(f32[256,384]{0,1:T(8,128)S(1)} %get-tuple-element.66), channel_id=1, source_target_pairs={{0,1},{1,2},{2,3},{3,4},{4,5},{5,6},{6,7},{7,8},{8,9},{9,10},{10,1... | collective-permute-start | bytes 1179656 | tf_op jit(solution)/shard_map/ppermute | solution.py:18
  266.4 10.6 %collective-permute-start.11 = (f32[256,384]{0,1:T(8,128)S(1)}, f32[256,384]{0,1:T(8,128)S(1)}, u32[]{:S(2)}, u32[]{:S(2)}) collective-permute-start(f32[256,384]{0,1:T(8,128)S(1)} %get-tuple-element.35), channel_id=1, source_target_pairs={{1,0},{2,1},{3,2},{4,3},{5,4},{6,5},{7,6},{8,7},{9,8},{10,9},{11,1... | collective-permute-start | bytes 1179656 | tf_op jit(solution)/shard_map/ppermute | solution.py:18
  277.3 8.9 %collective-permute-start.10 = (f32[256,384]{0,1:T(8,128)S(1)}, f32[256,384]{0,1:T(8,128)S(1)}, u32[]{:S(2)}, u32[]{:S(2)}) collective-permute-start(f32[256,384]{0,1:T(8,128)S(1)} %get-tuple-element.64), channel_id=1, source_target_pairs={{0,1},{1,2},{2,3},{3,4},{4,5},{5,6},{6,7},{7,8},{8,9},{9,10},{10,1... | collective-permute-start | bytes 1179656 | tf_op jit(solution)/shard_map/ppermute | solution.py:18
  311.5 25.9 %all-to-all-start.7 = ((f32[8,128,384]{2,1,0:T(8,128)}), f32[8,128,384]{2,1,0:T(8,128)}, u32[]{:S(2)}, u32[]{:S(2)}) async-start(f32[8,128,384]{2,1,0:T(8,128)} %broadcast_in_dim.148), calls=%async_computation.7 | async-start | bytes 3145728 | tf_op jit(solution)/shard_map/all_to_all | solution.py:42
  365.0 11.7 %collective-permute-start.13 = (f32[256,384]{0,1:T(8,128)S(1)}, f32[256,384]{0,1:T(8,128)S(1)}, u32[]{:S(2)}, u32[]{:S(2)}) collective-permute-start(f32[256,384]{0,1:T(8,128)S(1)} %get-tuple-element.31), channel_id=1, source_target_pairs={{1,0},{2,1},{3,2},{4,3},{5,4},{6,5},{7,6},{8,7},{9,8},{10,9},{11,1... | collective-permute-start | bytes 1179656 | tf_op jit(solution)/shard_map/ppermute | solution.py:18
  387.4 10.6 %collective-permute-start.15 = (f32[256,384]{0,1:T(8,128)S(1)}, f32[256,384]{0,1:T(8,128)S(1)}, u32[]{:S(2)}, u32[]{:S(2)}) collective-permute-start(f32[256,384]{0,1:T(8,128)S(1)} %get-tuple-element.25), channel_id=1, source_target_pairs={{1,0},{2,1},{3,2},{4,3},{5,4},{6,5},{7,6},{8,7},{9,8},{10,9},{11,1... | collective-permute-start | bytes 1179656 | tf_op jit(solution)/shard_map/ppermute | solution.py:18
  398.3 8.9 %collective-permute-start.14 = (f32[256,384]{0,1:T(8,128)S(1)}, f32[256,384]{0,1:T(8,128)S(1)}, u32[]{:S(2)}, u32[]{:S(2)}) collective-permute-start(f32[256,384]{0,1:T(8,128)S(1)} %get-tuple-element.60), channel_id=1, source_target_pairs={{0,1},{1,2},{2,3},{3,4},{4,5},{5,6},{6,7},{7,8},{8,9},{9,10},{10,1... | collective-permute-start | bytes 1179656 | tf_op jit(solution)/shard_map/ppermute | solution.py:18
  431.9 25.9 %all-to-all-start.10 = ((f32[8,128,384]{2,1,0:T(8,128)}), f32[8,128,384]{2,1,0:T(8,128)}, u32[]{:S(2)}, u32[]{:S(2)}) async-start(f32[8,128,384]{2,1,0:T(8,128)} %broadcast_in_dim.150), calls=%async_computation.10 | async-start | bytes 3145728 | tf_op jit(solution)/shard_map/all_to_all | solution.py:42
  483.9 11.7 %collective-permute-start.17 = (f32[256,384]{0,1:T(8,128)S(1)}, f32[256,384]{0,1:T(8,128)S(1)}, u32[]{:S(2)}, u32[]{:S(2)}) collective-permute-start(f32[256,384]{0,1:T(8,128)S(1)} %get-tuple-element.21), channel_id=1, source_target_pairs={{1,0},{2,1},{3,2},{4,3},{5,4},{6,5},{7,6},{8,7},{9,8},{10,9},{11,1... | collective-permute-start | bytes 1179656 | tf_op jit(solution)/shard_map/ppermute | solution.py:18
  495.9 9.0 %collective-permute-start.16 = (f32[256,384]{0,1:T(8,128)S(1)}, f32[256,384]{0,1:T(8,128)S(1)}, u32[]{:S(2)}, u32[]{:S(2)}) collective-permute-start(f32[256,384]{0,1:T(8,128)S(1)} %get-tuple-element.58), channel_id=1, source_target_pairs={{0,1},{1,2},{2,3},{3,4},{4,5},{5,6},{6,7},{7,8},{8,9},{9,10},{10,1... | collective-permute-start | bytes 1179656 | tf_op jit(solution)/shard_map/ppermute | solution.py:18
  506.6 10.6 %collective-permute-start.19 = (f32[256,384]{0,1:T(8,128)S(1)}, f32[256,384]{0,1:T(8,128)S(1)}, u32[]{:S(2)}, u32[]{:S(2)}) collective-permute-start(f32[256,384]{0,1:T(8,128)S(1)} %get-tuple-element.15), channel_id=1, source_target_pairs={{1,0},{2,1},{3,2},{4,3},{5,4},{6,5},{7,6},{8,7},{9,8},{10,9},{11,1... | collective-permute-start | bytes 1179656 | tf_op jit(solution)/shard_map/ppermute | solution.py:18
  518.3 9.2 %collective-permute-start.18 = (f32[256,384]{0,1:T(8,128)}, f32[256,384]{0,1:T(8,128)}, u32[]{:S(2)}, u32[]{:S(2)}) collective-permute-start(f32[256,384]{0,1:T(8,128)} %get-tuple-element.56), channel_id=1, source_target_pairs={{0,1},{1,2},{2,3},{3,4},{4,5},{5,6},{6,7},{7,8},{8,9},{9,10},{10,1... | collective-permute-start | bytes 1179656 | tf_op jit(solution)/shard_map/ppermute | solution.py:18
  (82 other events, 453.0 us)
where the time goes:
time: 541 us; the launch traced here: 533 us
  waiting for transfers between devices  206 us (38%)
  blocking collectives  135 us (25%)
  starting transfers between devices  74.7 us (14%)
  other arithmetic  42.3 us (8%)
  local copies, waits for them, and re-layouts  36.1 us (7%)
  matrix products  33 us (6%)
  between operations  6.04 us (1%)
    ppermute x18, waiting for transfers between devices, from_behind(): return lax.ppermute(block, axis, route)  126 us
    all_to_all x5, waiting for transfers between devices, from_everyone(): return lax.all_to_all(copies, axis, split_axis=0, concat_axis=0, tiled=True)  80.3 us
    all_to_all x4, blocking collectives, on_device(): lax.all_to_all(partial_vals, 'sub', split_axis=0, concat_axis=0, tiled=True)  70.9 us
    all_to_all x3, blocking collectives, from_everyone(): return lax.all_to_all(copies, axis, split_axis=0, concat_axis=0, tiled=True)  64.5 us
    ppermute x18, starting transfers between devices, from_behind(): return lax.ppermute(block, axis, route)  41 us
    all_to_all x5, starting transfers between devices, from_everyone(): return lax.all_to_all(copies, axis, split_axis=0, concat_axis=0, tiled=True)  27.3 us
    unnamed x164, local copies, waits for them, and re-layouts  16.8 us
  transfers between devices with their start and end apart: 25, of which 22 were waited for; matrix products, arithmetic and copies ran while one was open for 6% of the time, Pallas kernels for 0%

commit v1 on v0

v1 whole, which is shorter than its diff:
```python
import functools
import math

import jax
import jax.numpy as jnp
from jax import lax
from jax.experimental import pallas as pl
from jax.experimental.pallas import tpu as pltpu
from jax.sharding import PartitionSpec as P

ITERS = 4
OMEGA = 0.6
SH = 256
COLS = 128
CORES = 2
STIFF_LANE = 64
F32 = jnp.float32
BF16 = jnp.bfloat16
BY_ROWS = (((1,), (1,)), ((), ()))


def iota(shape, dim):
    return lax.broadcasted_iota(jnp.int32, shape, dim)


def kernel(
    nx, nz, ny, chunks,
    share, info, loads_hbm, schur_hbm, neumann_hbm, basis_hbm, coarse_hbm,
    sol_hbm, res_hbm,
    schur, neumann, basis, coarse, halves,
    loads, local, field, sol, weighted, rounded,
    from_lower, from_upper, corr_lower, corr_upper,
    weight_head, weight_tail, perm,
    edge_out, edge_in, extended, extended_t,
    pick_rows, select, chosen, columns, columns_hl, coarse_k,
    terms, part_y, got_y, part_z, got_z, picked, picked_near,
    loc_sem, out_sem,
    h1s, h1r, h2s, h2r, nps, npr, xs, xr, cs, cr, ys, yr, zs, zr,
    gzs, gzr, gxs, gxr, gcs, gcr, bs, br,
):
    half = nz // CORES
    subs = nx * nz
    unknowns = loads.shape[1]
    ncl = basis.shape[0]
    order = coarse.shape[1]
    own_rows = coarse.shape[0]
    tail0 = unknowns - SH
    tiles = unknowns // SH
    edges = (0, tiles - 1)
    inner = tuple(range(1, tiles - 1))

    g, s = lax.axis_index("group"), lax.axis_index("sub")
    y, c = g // CORES, g % CORES
    z, x = s // nx, s % nx
    upper = (g, lax.rem(s + 1, subs))
    lower = (g, lax.rem(s + subs - 1, subs))
    x_peers = [(g, z * nx + lax.rem(x + d, nx)) for d in range(1, nx)]
    z_peers = [(g, lax.rem(z + d, nz) * nx + x) for d in range(1, nz)]
    y_peers = [(lax.rem(y + d, ny) * CORES + c, s) for d in range(1, ny)]
    core_peer = (y * CORES + 1 - c, s)

    share_low, share_up = share[0], share[1]

    def remote(src, dst, send, recv, to):
        return pltpu.make_async_remote_copy(
            src_ref=src, dst_ref=dst, send_sem=send, recv_sem=recv,
            device_id=to, device_id_type=pl.DeviceIdType.MESH,
        )

    def start(copies):
        for copy in copies:
            copy.start()

    def landed(copies):
        for copy in copies:
            copy.wait_recv()

    def sent(copies):
        for copy in copies:
            copy.wait_send()

    def rows(tile):
        return pl.ds(tile * SH, SH)

    def halo_local(ch):
        return (
            remote(local.at[ch, pl.ds(tail0, SH)], from_lower.at[ch], h1s.at[ch, 0], h1r.at[ch, 0], upper),
            remote(local.at[ch, pl.ds(0, SH)], from_upper.at[ch], h1s.at[ch, 1], h1r.at[ch, 1], lower),
        )

    def halo_field(ch):
        return (
            remote(field.at[ch, pl.ds(tail0, SH)], corr_lower.at[ch], h2s.at[ch, 0], h2r.at[ch, 0], upper),
            remote(field.at[ch, pl.ds(0, SH)], corr_upper.at[ch], h2s.at[ch, 1], h2r.at[ch, 1], lower),
        )

    def terms_x(k, ch):
        own = terms.at[k, ch, c, x]
        return [remote(own, own, xs.at[ch, d], xr.at[k, ch, d], to) for d, to in enumerate(x_peers)]

    def terms_core(k, ch):
        own = terms.at[k, ch, c]
        return (remote(own, own, cs.at[ch], cr.at[k, ch], core_peer),)

    def parts_y(k, ch):
        return [
            remote(part_y.at[ch, lax.rem(y + d + 1, ny)], got_y.at[k, ch, d], ys.at[ch, d], yr.at[k, ch, d], to)
            for d, to in enumerate(y_peers)
        ]

    def parts_z(k, ch):
        return [
            remote(part_z.at[ch, lax.rem(z + d + 1, nz)], got_z.at[k, ch, d], zs.at[ch, d], zr.at[k, ch, d], to)
            for d, to in enumerate(z_peers)
        ]

    def picked_halo(ch):
        return (
            remote(picked.at[ch], picked_near.at[ch, 0], nps.at[ch, 0], npr.at[ch, 0], upper),
            remote(picked.at[ch], picked_near.at[ch, 1], nps.at[ch, 1], npr.at[ch, 1], lower),
        )

    def basis_halo():
        return (
            remote(edge_out.at[0], edge_in.at[0], bs.at[0], br.at[0], upper),
            remote(edge_out.at[1], edge_in.at[1], bs.at[1], br.at[1], lower),
        )

    def columns_z():
        return [
            remote(chosen.at[lax.rem(z + d + 1, nz)], columns.at[c, x, lax.rem(z, half)], gzs.at[d], gzr.at[d], to)
            for d, to in enumerate(z_peers)
        ]

    def columns_x():
        own = columns.at[c, x]
        return [remote(own, own, gxs.at[d], gxr.at[d], to) for d, to in enumerate(x_peers)]

    def columns_core():
        own = columns.at[c]
        return (remote(own, own, gcs.at[0], gcr.at[0], core_peer),)

    load_in = [
        pltpu.make_async_copy(loads_hbm.at[:, pl.ds(ch * COLS, COLS)], loads.at[ch], loc_sem.at[ch])
        for ch in range(chunks)
    ]
    others = [
        pltpu.make_async_copy(src, dst, loc_sem.at[chunks + i])
        for i, (src, dst) in enumerate(
            ((basis_hbm, basis), (coarse_hbm, coarse), (neumann_hbm, neumann), (schur_hbm, schur))
        )
    ]
    start(load_in)
    start(others)
    barrier = pltpu.get_barrier_semaphore()
    peers = [upper, lower, *x_peers, *z_peers, *y_peers, core_peer]
    for peer in peers:
        pl.semaphore_signal(barrier, inc=1, device_id=peer, device_id_type=pl.DeviceIdType.MESH)
    pl.semaphore_wait(barrier, len(peers))

    turn = lax.rem(share_up, SH)
    turn_back = lax.rem(2 * SH - share_up, SH)
    for ch in range(chunks):
        load_in[ch].wait()
        loads[ch, tail0:, :] = pltpu.roll(loads[ch, tail0:, :], turn, axis=0)
        local[ch, :, :] = loads[ch, :, :]
        start(halo_local(ch))

    def stiffness_of(sub):
        row = info[pl.ds(g * subs + sub, 1), :]
        lane = iota((1, COLS), 1)
        return jnp.sum(jnp.where(lane == STIFF_LANE, row, 0.0), axis=1, keepdims=True)

    own_stiff = stiffness_of(s)
    low_stiff = stiffness_of(lower[1])
    up_stiff = stiffness_of(upper[1])
    w_low = own_stiff / (own_stiff + low_stiff)
    w_up = own_stiff / (own_stiff + up_stiff)
    n_low = low_stiff / (low_stiff + own_stiff)
    n_up = up_stiff / (up_stiff + own_stiff)
    in_low = iota((SH, COLS), 0) < share_low
    in_up = iota((SH, COLS), 0) < share_up
    weight_head[...] = jnp.where(in_low, w_low, 1.0)
    weight_tail[...] = jnp.where(in_up, w_up, 1.0)

    moved = (iota((SH, SH), 0) + (SH - share_up)) & (SH - 1)
    perm[...] = jnp.where(iota((SH, SH), 1) == moved, 1.0, 0.0).astype(BF16)
    others[0].wait()
    basis_tail = lax.dot_general(basis[:, tail0:], perm[...], BY_ROWS, preferred_element_type=F32)
    basis[:, tail0:] = basis_tail.astype(BF16)
    edge_out[0] = basis_tail
    edge_out[1] = basis[:, :SH].astype(F32)
    start(basis_halo())
    lane_low = iota((ncl, SH), 1) < share_low
    lane_up = iota((ncl, SH), 1) < share_up
    extended[...] = jnp.zeros_like(extended)
    extended[0:ncl, :] = basis[...].astype(F32)
    extended[0:ncl, :SH] = jnp.where(lane_low, w_low, 1.0) * extended[0:ncl, :SH]
    extended[0:ncl, tail0:] = jnp.where(lane_up, w_up, 1.0) * extended[0:ncl, tail0:]

    def dof_column(device):
        row = jnp.broadcast_to(info[pl.ds(device, 1), :], (ncl, COLS))
        hit = iota((ncl, COLS), 0) == iota((ncl, COLS), 1)
        return jnp.sum(jnp.where(hit, row, 0.0), axis=1, keepdims=True).astype(jnp.int32)

    others[1].wait()
    high = coarse[...].astype(BF16)
    halves[0:own_rows, :] = high
    halves[own_rows:, :] = (coarse[...] - high.astype(F32)).astype(BF16)

    def choose(zt, carry):
        for cc in range(CORES):
            for xx in range(nx):
                column = dof_column((y * CORES + cc) * subs + zt * nx + xx)
                at = (cc * nx + xx) * ncl
                select[at : at + ncl, :] = jnp.where(iota((ncl, order), 1) == column, 1.0, 0.0).astype(BF16)
        both = lax.dot_general(select[...], halves[...], BY_ROWS, preferred_element_type=F32)
        chosen[zt] = both[:, :own_rows] + both[:, own_rows:]
        return carry

    lax.fori_loop(0, nz, choose, 0)

    sends_here = z // half == c

    @pl.when(sends_here)
    def _():
        start(columns_z())
        columns[c, x, lax.rem(z, half)] = chosen[z]

    for yy in range(ny):
        for zz in range(nz):
            column = jnp.broadcast_to(dof_column((yy * CORES + c) * subs + zz * nx + x), (ncl, order))
            at = (yy * nz + zz) * ncl
            pick_rows[at : at + ncl, :] = jnp.where(iota((ncl, order), 1) == column, 1.0, 0.0).astype(BF16)

    def align(matrix):
        wide = jnp.dot(perm[...], matrix[tail0:, :], preferred_element_type=F32)
        matrix[tail0:, :] = wide.astype(BF16)

        def turn_columns(tile, carry):
            at = pl.ds(pl.multiple_of(tile * SH, SH), SH)
            swapped = lax.dot_general(matrix[at, tail0:], perm[...], BY_ROWS, preferred_element_type=F32)
            matrix[at, tail0:] = swapped.astype(BF16)
            return carry

        lax.fori_loop(0, tiles, turn_columns, 0)

    others[2].wait()
    align(neumann)

    for d, copy in enumerate(columns_z()):
        sender = lax.rem(z + nz - 1 - d, nz)
        pl.when(sender // half == c)(copy.wait_recv)
    start(columns_x())

    others[3].wait()
    align(schur)

    @pl.when(sends_here)
    def _():
        sent(columns_z())

    sol[...] = jnp.zeros_like(sol)

    def each_chunk(step):
        def body(ch, carry):
            step(ch)
            return carry

        lax.fori_loop(0, chunks, body, 0)

    def weigh(k, ch):
        landed(halo_local(ch))
        head = local[ch, :SH, :] + jnp.where(in_low, from_lower[ch], 0.0)
        weighted[ch, :SH, :] = (weight_head[...] * head).astype(BF16)
        weighted[ch, SH:tail0, :] = local[ch, SH:tail0, :].astype(BF16)
        tail = local[ch, tail0:, :] + jnp.where(in_up, from_upper[ch], 0.0)
        weighted[ch, tail0:, :] = (weight_tail[...] * tail).astype(BF16)
        terms[k, ch, c, x] = jnp.dot(basis[...], weighted[ch], preferred_element_type=F32)
        start(terms_x(k, ch))
        for tile in edges + inner:
            product = jnp.dot(neumann[rows(tile), :], weighted[ch], preferred_element_type=F32)
            if tile == 0:
                product = weight_head[...] * product
            if tile == tiles - 1:
                product = weight_tail[...] * product
            field[ch, rows(tile), :] = product
            if tile == edges[-1]:
                start(halo_field(ch))

    def to_core(k, ch):
        landed(terms_x(k, ch))
        start(terms_core(k, ch))

    def solve(k, ch):
        landed(terms_core(k, ch))
        mine = terms[k, ch].reshape(CORES * nx * ncl, COLS)
        high = mine.astype(BF16)
        low = (mine - high.astype(F32)).astype(BF16)
        stacked = jnp.concatenate([high, high, low], axis=0)
        solved = jnp.dot(coarse_k[...], stacked, preferred_element_type=F32)
        part_y[ch] = solved.reshape(ny, nz * ncl, COLS)
        start(parts_y(k, ch))

    def sum_y(k, ch):
        copies = parts_y(k, ch)
        landed(copies)
        total = part_y[ch, y]
        for d in range(ny - 1):
            total = total + got_y[k, ch, d]
        part_z[ch] = total.reshape(nz, ncl, COLS)
        start(parts_z(k, ch))
        sent(copies)

    def sum_z(k, ch):
        copies = parts_z(k, ch)
        landed(copies)
        total = part_z[ch, z]
        for d in range(nz - 1):
            total = total + got_z[k, ch, d]
        picked[ch] = total
        start(picked_halo(ch))
        sent(copies)

    def advance(k, ch):
        near = picked_halo(ch)
        landed(near)
        halo = halo_field(ch)
        landed(halo)
        stacked = jnp.concatenate(
            [picked[ch], picked_near[ch, 0], picked_near[ch, 1], jnp.zeros((COLS - 3 * ncl, COLS), F32)], axis=0
        ).astype(BF16)
        sent(near)
        sent(halo)
        for tile in range(tiles):
            change = field[ch, rows(tile), :] + jnp.dot(
                extended_t[rows(tile), :], stacked, preferred_element_type=F32
            )
            if tile == 0:
                change = change + jnp.where(in_low, corr_lower[ch], 0.0)
            if tile == tiles - 1:
                change = change + jnp.where(in_up, corr_upper[ch], 0.0)
            new = sol[ch, rows(tile), :] + OMEGA * change
            sol[ch, rows(tile), :] = new
            rounded[rows(tile), :] = new.astype(BF16)
        out = halo_local(ch)
        sent(out)
        for tile in edges + inner:
            product = jnp.dot(schur[rows(tile), :], rounded[...], preferred_element_type=F32)
            local[ch, rows(tile), :] = loads[ch, rows(tile), :] - product
            if tile == edges[-1]:
                start(out)
        sent(terms_x(k, ch))
        sent(terms_core(k, ch))

    def finish_setup():
        copies = columns_x()
        landed(copies)
        start(columns_core())
        sent(copies)
        edge = basis_halo()
        landed(edge)
        extended[ncl : 2 * ncl, :SH] = jnp.where(lane_low, n_low * edge_in[0], 0.0)
        extended[2 * ncl : 3 * ncl, tail0:] = jnp.where(lane_up, n_up * edge_in[1], 0.0)
        extended_t[...] = extended[...].T.astype(BF16)
        sent(edge)
        landed(columns_core())
        wide = CORES * nx * ncl
        for cc in range(CORES):
            for xx in range(nx):
                for i in range(half):
                    block = columns[cc, xx, i]
                    high = block.astype(BF16)
                    at = ((cc * half + i) * nx + xx) * own_rows
                    columns_hl[:wide, at : at + own_rows] = high
                    columns_hl[wide:, at : at + own_rows] = (block - high.astype(F32)).astype(BF16)

        def row_tile(tile, carry):
            at = pl.ds(pl.multiple_of(tile * COLS, COLS), COLS)
            both = lax.dot_general(pick_rows[at, :], columns_hl[...], BY_ROWS, preferred_element_type=F32)
            high = both[:, :wide].astype(BF16)
            coarse_k[at, :wide] = high
            coarse_k[at, wide : 2 * wide] = both[:, wide:].astype(BF16)
            coarse_k[at, 2 * wide :] = high
            return carry

        lax.fori_loop(0, pick_rows.shape[0] // COLS, row_tile, 0)
        sent(columns_core())

    def iteration(k, carry):
        each_chunk(functools.partial(weigh, k))
        each_chunk(functools.partial(to_core, k))
        pl.when(k == 0)(finish_setup)
        each_chunk(functools.partial(solve, k))
        each_chunk(functools.partial(sum_y, k))
        each_chunk(functools.partial(sum_z, k))
        each_chunk(functools.partial(advance, k))
        return carry

    lax.fori_loop(0, ITERS, iteration, 0)

    out_copies = []
    for ch in range(chunks):
        sol[ch, tail0:, :] = pltpu.roll(sol[ch, tail0:, :], turn_back, axis=0)
        copy = pltpu.make_async_copy(sol.at[ch], sol_hbm.at[:, pl.ds(ch * COLS, COLS)], out_sem.at[ch])
        copy.start()
        out_copies.append(copy)
    for ch in range(chunks):
        copies = halo_local(ch)
        landed(copies)
        field[ch, :SH, :] = local[ch, :SH, :] + jnp.where(in_low, from_lower[ch], 0.0)
        field[ch, SH:tail0, :] = local[ch, SH:tail0, :]
        tail = local[ch, tail0:, :] + jnp.where(in_up, from_upper[ch], 0.0)
        field[ch, tail0:, :] = pltpu.roll(tail, turn_back, axis=0)
        copy = pltpu.make_async_copy(field.at[ch], res_hbm.at[:, pl.ds(ch * COLS, COLS)], out_sem.at[chunks + ch])
        copy.start()
        out_copies.append(copy)
        sent(copies)
    for copy in out_copies:
        copy.wait()


def on_device(
    shared_sizes,
    stiffness,
    load_cases,
    schur_blocks,
    neumann_inverse,
    coarse_basis,
    coarse_dofs,
    coarse_inverse,
):
    groups, subs = lax.axis_size("group"), lax.axis_size("sub")
    nx = math.isqrt(subs)
    nz, ny = subs // nx, groups // CORES
    half = nz // CORES
    unknowns, cases = load_cases.shape[2:]
    chunks = cases // COLS
    ncl = coarse_basis.shape[2]
    own_rows, order = coarse_inverse.shape
    wide, tall = CORES * nx * ncl, ny * nz * ncl

    mine = jnp.zeros((1, COLS), F32)
    mine = mine.at[:, :ncl].set(coarse_dofs[0].astype(F32))
    mine = mine.at[:, STIFF_LANE].set(stiffness[0])
    info = lax.all_gather(mine, ("group", "sub"), axis=0, tiled=True)

    dma = pltpu.SemaphoreType.DMA
    vmem = pltpu.VMEM
    scratch = [
        vmem((unknowns, unknowns), BF16),
        vmem((unknowns, unknowns), BF16),
        vmem((ncl, unknowns), BF16),
        vmem((own_rows, order), F32),
        vmem((2 * own_rows, order), BF16),
        vmem((chunks, unknowns, COLS), F32),
        vmem((chunks, unknowns, COLS), F32),
        vmem((chunks, unknowns, COLS), F32),
        vmem((chunks, unknowns, COLS), F32),
        vmem((chunks, unknowns, COLS), BF16),
        vmem((unknowns, COLS), BF16),
        vmem((chunks, SH, COLS), F32),
        vmem((chunks, SH, COLS), F32),
        vmem((chunks, SH, COLS), F32),
        vmem((chunks, SH, COLS), F32),
        vmem((SH, COLS), F32),
        vmem((SH, COLS), F32),
        vmem((SH, SH), BF16),
        vmem((2, ncl, SH), F32),
        vmem((2, ncl, SH), F32),
        vmem((COLS, unknowns), F32),
        vmem((unknowns, COLS), BF16),
        vmem((tall, order), BF16),
        vmem((wide, order), BF16),
        vmem((nz, wide, own_rows), F32),
        vmem((CORES, nx, half, wide, own_rows), F32),
        vmem((2 * wide, order), BF16),
        vmem((tall, 3 * wide), BF16),
        vmem((ITERS, chunks, CORES, nx, ncl, COLS), F32),
        vmem((chunks, ny, nz * ncl, COLS), F32),
        vmem((ITERS, chunks, ny - 1, nz * ncl, COLS), F32),
        vmem((chunks, nz, ncl, COLS), F32),
        vmem((ITERS, chunks, nz - 1, ncl, COLS), F32),
        vmem((chunks, ncl, COLS), F32),
        vmem((chunks, 2, ncl, COLS), F32),
        dma((chunks + 4,)),
        dma((2 * chunks,)),
        dma((chunks, 2)), dma((chunks, 2)),
        dma((chunks, 2)), dma((chunks, 2)),
        dma((chunks, 2)), dma((chunks, 2)),
        dma((chunks, nx - 1)), dma((ITERS, chunks, nx - 1)),
        dma((chunks,)), dma((ITERS, chunks)),
        dma((chunks, ny - 1)), dma((ITERS, chunks, ny - 1)),
        dma((chunks, nz - 1)), dma((ITERS, chunks, nz - 1)),
        dma((nz - 1,)), dma((nz - 1,)),
        dma((nx - 1,)), dma((nx - 1,)),
        dma((1,)), dma((1,)),
        dma((2,)), dma((2,)),
    ]
    anywhere = pl.BlockSpec(memory_space=pl.ANY)
    out = jax.ShapeDtypeStruct((unknowns, cases), F32)
    sol, res = pl.pallas_call(
        functools.partial(kernel, nx, nz, ny, chunks),
        out_shape=(out, out),
        in_specs=[pl.BlockSpec(memory_space=pltpu.SMEM), pl.BlockSpec(memory_space=pltpu.VMEM)] + [anywhere] * 5,
        out_specs=(anywhere, anywhere),
        scratch_shapes=scratch,
        compiler_params=pltpu.CompilerParams(
            collective_id=0, has_side_effects=True, vmem_limit_bytes=56 * 1024 * 1024
        ),
        cost_estimate=pl.CostEstimate(flops=2 * 9 * unknowns * unknowns * cases, bytes_accessed=1 << 24, transcendentals=0),
    )(
        shared_sizes[0, 0],
        info,
        load_cases[0, 0],
        schur_blocks[0, 0],
        neumann_inverse[0, 0],
        coarse_basis[0, 0],
        coarse_inverse,
    )
    return (sol[None, None], res[None, None])


def solution(mesh):
    return jax.shard_map(
        on_device,
        mesh=mesh,
        in_specs=(
            P("group", "sub", None),
            P("group", "sub"),
            P("group", "sub", None, None),
            P("group", "sub", None, None),
            P("group", "sub", None, None),
            P("group", "sub", None, None),
            P("group", "sub", None),
            P("sub", None),
        ),
        out_specs=(P("group", "sub", None, None), P("group", "sub", None, None)),
        check_vma=False,
    )
```

time: 541 us -> 228 us (0.42); the launches traced: 533 us -> 228 us
  waiting for transfers between devices: 206 us -> 0 us
  Pallas kernels: 0 us -> 171 us
  blocking collectives: 135 us -> 48.5 us
  starting transfers between devices: 74.7 us -> 0 us
  other arithmetic: 42.3 us -> 2.58 us
  matrix products: 33 us -> 0 us
  local copies, waits for them, and re-layouts: 36.1 us -> 4.02 us
    pallas_call x0 -> x1, Pallas kernels: none -> 171 us  [on_device(): pl.pallas_call(functools.partial(kernel, nx, nz, ny, chunks), out_shape=(...]
    all_to_all x7 -> x0, blocking collectives: 135 us -> none  [the longest x4 70.9 us: on_device(): lax.all_to_all(partial_vals, 'sub', split_axis=0, concat_axis=0, tiled=True)]
    ppermute x20 -> x0, waiting for transfers between devices: 126 us -> none  [the longest x18 126 us: from_behind(): return lax.ppermute(block, axis, route)]
    all_to_all x5 -> x0, waiting for transfers between devices: 80.3 us -> none  [from_everyone(): return lax.all_to_all(copies, axis, split_axis=0, concat_axis=0, tiled=True)]
    all_gather x0 -> x1, blocking collectives: none -> 48.5 us  [on_device(): info = lax.all_gather(mine, ('group', 'sub'), axis=0, tiled=True)]
    ppermute x20 -> x0, starting transfers between devices: 47.4 us -> none  [the longest x18 41 us: from_behind(): return lax.ppermute(block, axis, route)]
    dot_general x25 -> x0, matrix products: 33 us -> none  [the longest x4 10.6 us: on_device(): correction = jnp.dot(neumann, weighted, preferred_element_type=jnp.float32)]
    all_to_all x5 -> x0, starting transfers between devices: 27.3 us -> none  [from_everyone(): return lax.all_to_all(copies, axis, split_axis=0, concat_axis=0, tiled=True)]
  transfers between devices with their start and end apart: 25 -> 0, of which waited for: 22 -> 0; matrix products, arithmetic and copies ran while one was open for 6% -> 0% of each run, Pallas kernels for 0% -> 0%
where the time goes in v1:
time: 228 us
  Pallas kernels  171 us (75%)
  blocking collectives  48.5 us (21%)
  local copies, waits for them, and re-layouts  4.02 us (2%)
  other arithmetic  2.58 us (1%)
    pallas_call x1, Pallas kernels, on_device(): pl.pallas_call(functools.partial(kernel, nx, nz, ny, chunks), out_shape=(...  171 us
    all_gather x1, blocking collectives, on_device(): info = lax.all_gather(mine, ('group', 'sub'), axis=0, tiled=True)  48.5 us

profile of v1, /device:TPU:0, one launch (start us, length us, event | category | flops | bytes accessed | tf_op | source)
XLA Modules:
  0.0 227.7 jit_solution(6935448917521237562)
XLA Ops:
  0.6 0.6 compare_reduce_fusion.1
  1.3 0.6 compare_reduce_fusion
  3.2 1.3 fusion
  4.5 0.1 scatter.12
  4.6 48.5 %all-gather = f32[128,1,128]{2,1,0:T(1,128)} all-gather(f32[1,1,128]{2,1,0:T(1,128)S(1)} %scatter.12), channel_id=1, replica_groups=mesh['group'=8,'sub'=16] {'group','sub'}, dimensions={0}, use_global_device_ids=true | all-gather | bytes 66048 | tf_op jit(solution)/shard_map/all_gather | solution.py:446
  53.1 170.7 %shard_map.95 = (f32[1024,384]{1,0:T(8,128)}, f32[1024,384]{1,0:T(8,128)}) custom-call(s32[2]{0:T(128)} %bitcast.21, f32[128,128]{1,0:T(8,128)} %bitcast.16, f32[1024,384]{1,0:T(8,128)} %bitcast.19, bf16[1024,1024]{1,0:T(8,128)(2,1)} %bitcast.17, bf16[1024,1024]{1,0:T(8,128)(2,1)} %bitcast.18, bf16[32,1024]{1,0:T(8,128)(2,1)} %bitcast.20, f32[128,2048]{1,0:T(8,128)} %coarse_hbm.1), custom_call_target="tpu_custom_call" | custom-call | flops 7247757312 | bytes 16777216 | tf_op jit(solution)/shard_map/pallas_call | solution.py:502
  223.8 0.0 copy-start
  223.8 2.8 %copy.15 = f32[1,1,1024,384]{3,2,1,0:T(8,128)} copy(f32[1,1,1024,384]{3,2,1,0:T(8,128)} %bitcast.15) | data formatting | bytes 3145728
  226.6 0.0 copy-done
  226.6 1.1 copy.16
  (1 shorter events, 0.0 us)
Async XLA Ops:
  223.8 2.8 %copy-start = (f32[1024,384]{1,0:T(8,128)S(1)}, f32[1024,384]{1,0:T(8,128)}, u32[]{:S(2)}) copy-start(f32[1024,384]{1,0:T(8,128)} %get-tuple-element.29) | copy-start | bytes 4718596

commit v2 on v1

--- a/solution.py
+++ b/solution.py
@@ -13,10 +13,8 @@
 SH = 256
 COLS = 128
 CORES = 2
-STIFF_LANE = 64
 F32 = jnp.float32
 BF16 = jnp.bfloat16
-BY_ROWS = (((1,), (1,)), ((), ()))
 
 
 def iota(shape, dim):
@@ -25,18 +23,20 @@
 
 def kernel(
     nx, nz, ny, chunks,
-    share, info, loads_hbm, schur_hbm, neumann_hbm, basis_hbm, coarse_hbm,
+    share, stiff, dofs, loads_hbm, schur_hbm, neumann_hbm, basis_hbm, coarse_hbm,
     sol_hbm, res_hbm,
     schur, neumann, basis, coarse, halves,
     loads, local, field, sol, weighted, rounded,
     from_lower, from_upper, corr_lower, corr_upper,
-    weight_head, weight_tail, perm,
+    weight_head, weight_tail, perm, perm_t,
     edge_out, edge_in, extended, extended_t,
     pick_rows, select, chosen, columns, columns_hl, coarse_k,
-    terms, part_y, got_y, part_z, got_z, picked, picked_near,
+    terms, part_y, got_y, part_z, got_z, near_z,
+    facts, facts_near, facts_far, facts_side,
     loc_sem, out_sem,
     h1s, h1r, h2s, h2r, nps, npr, xs, xr, cs, cr, ys, yr, zs, zr,
     gzs, gzr, gxs, gxr, gcs, gcr, bs, br,
+    fxs, fxr, fcs, fcr, fzs, fzr, fbs, fbr, fys, fyr, fns, fnr,
 ):
     half = nz // CORES
     subs = nx * nz
@@ -56,6 +56,8 @@
     lower = (g, lax.rem(s + subs - 1, subs))
     x_peers = [(g, z * nx + lax.rem(x + d, nx)) for d in range(1, nx)]
     z_peers = [(g, lax.rem(z + d, nz) * nx + x) for d in range(1, nz)]
+    in_column = [lax.rem(z + d, nz) * nx + x for d in range(nz)]
+    beside = [[(g, lax.rem(sub + step, subs)) for sub in in_column] for step in (1, subs - 1)]
     y_peers = [(lax.rem(y + d, ny) * CORES + c, s) for d in range(1, ny)]
     core_peer = (y * CORES + 1 - c, s)
 
@@ -110,15 +112,19 @@
 
     def parts_z(k, ch):
         return [
-            remote(part_z.at[ch, lax.rem(z + d + 1, nz)], got_z.at[k, ch, d], zs.at[ch, d], zr.at[k, ch, d], to)
+            remote(part_z.at[ch, lax.rem(z + d + 1, nz)], got_z.at[k, ch, z], zs.at[ch, d], zr.at[k, ch, d], to)
             for d, to in enumerate(z_peers)
         ]
 
-    def picked_halo(ch):
-        return (
-            remote(picked.at[ch], picked_near.at[ch, 0], nps.at[ch, 0], npr.at[ch, 0], upper),
-            remote(picked.at[ch], picked_near.at[ch, 1], nps.at[ch, 1], npr.at[ch, 1], lower),
-        )
+    def parts_beside(k, ch):
+        return [
+            remote(
+                part_z.at[ch, lax.rem(z + d, nz)], near_z.at[k, ch, side, z],
+                nps.at[ch, side, d], npr.at[k, ch, side, d], beside[side][d],
+            )
+            for side in range(2)
+            for d in range(nz)
+        ]
 
     def basis_halo():
         return (
@@ -139,6 +145,31 @@
     def columns_core():
         own = columns.at[c]
         return (remote(own, own, gcs.at[0], gcr.at[0], core_peer),)
+
+    def facts_x():
+        own = facts_near.at[z, c, x]
+        return [remote(facts, own, fxs.at[d], fxr.at[d], to) for d, to in enumerate(x_peers)]
+
+    def facts_core():
+        own = facts_near.at[z, c]
+        return (remote(own, own, fcs.at[0], fcr.at[0], core_peer),)
+
+    def facts_z():
+        own = facts_near.at[z]
+        return [remote(own, own, fzs.at[d], fzr.at[d], to) for d, to in enumerate(z_peers)]
+
+    def far_z():
+        return [remote(facts, facts_far.at[y, z], fbs.at[d], fbr.at[d], to) for d, to in enumerate(z_peers)]
+
+    def far_y():
+        own = facts_far.at[y]
+        return [remote(own, own, fys.at[d], fyr.at[d], to) for d, to in enumerate(y_peers)]
+
+    def facts_beside():
+        return (
+            remote(facts, facts_side.at[0], fns.at[0], fnr.at[0], upper),
+            remote(facts, facts_side.at[1], fns.at[1], fnr.at[1], lower),
+        )
 
     load_in = [
         pltpu.make_async_copy(loads_hbm.at[:, pl.ds(ch * COLS, COLS)], loads.at[ch], loc_sem.at[ch])
@@ -152,11 +183,19 @@
     ]
     start(load_in)
     start(others)
+    facts[...] = jnp.full(facts.shape, stiff[0], F32)
+    facts[0:1, :ncl] = dofs[...].astype(F32)
+    facts_near[z, c, x] = facts[...]
+    facts_far[y, z] = facts[...]
     barrier = pltpu.get_barrier_semaphore()
-    peers = [upper, lower, *x_peers, *z_peers, *y_peers, core_peer]
+    peers = [*beside[0], *beside[1], *x_peers, *z_peers, *y_peers, core_peer]
     for peer in peers:
         pl.semaphore_signal(barrier, inc=1, device_id=peer, device_id_type=pl.DeviceIdType.MESH)
     pl.semaphore_wait(barrier, len(peers))
+
+    start(facts_beside())
+    start(facts_x())
+    start(far_z())
 
     turn = lax.rem(share_up, SH)
     turn_back = lax.rem(2 * SH - share_up, SH)
@@ -166,14 +205,14 @@
         local[ch, :, :] = loads[ch, :, :]
         start(halo_local(ch))
 
-    def stiffness_of(sub):
-        row = info[pl.ds(g * subs + sub, 1), :]
-        lane = iota((1, COLS), 1)
-        return jnp.sum(jnp.where(lane == STIFF_LANE, row, 0.0), axis=1, keepdims=True)
-
-    own_stiff = stiffness_of(s)
-    low_stiff = stiffness_of(lower[1])
-    up_stiff = stiffness_of(upper[1])
+    landed(facts_x())
+    start(facts_core())
+    landed(far_z())
+    start(far_y())
+    landed(facts_beside())
+    own_stiff = facts[1:2, 0:1]
+    low_stiff = facts_side[0, 1:2, 0:1]
+    up_stiff = facts_side[1, 1:2, 0:1]
     w_low = own_stiff / (own_stiff + low_stiff)
     w_up = own_stiff / (own_stiff + up_stiff)
     n_low = low_stiff / (low_stiff + own_stiff)
@@ -185,8 +224,10 @@
 
     moved = (iota((SH, SH), 0) + (SH - share_up)) & (SH - 1)
     perm[...] = jnp.where(iota((SH, SH), 1) == moved, 1.0, 0.0).astype(BF16)
+    moved_lane = (iota((SH, SH), 1) + (SH - share_up)) & (SH - 1)
+    perm_t[...] = jnp.where(iota((SH, SH), 0) == moved_lane, 1.0, 0.0).astype(BF16)
     others[0].wait()
-    basis_tail = lax.dot_general(basis[:, tail0:], perm[...], BY_ROWS, preferred_element_type=F32)
+    basis_tail = jnp.dot(basis[:, tail0:], perm_t[...], preferred_element_type=F32)
     basis[:, tail0:] = basis_tail.astype(BF16)
     edge_out[0] = basis_tail
     edge_out[1] = basis[:, :SH].astype(F32)
@@ -198,24 +239,33 @@
     extended[0:ncl, :SH] = jnp.where(lane_low, w_low, 1.0) * extended[0:ncl, :SH]
     extended[0:ncl, tail0:] = jnp.where(lane_up, w_up, 1.0) * extended[0:ncl, tail0:]
 
-    def dof_column(device):
-        row = jnp.broadcast_to(info[pl.ds(device, 1), :], (ncl, COLS))
+    def dof_column(row):
+        row = jnp.broadcast_to(row, (ncl, COLS))
         hit = iota((ncl, COLS), 0) == iota((ncl, COLS), 1)
         return jnp.sum(jnp.where(hit, row, 0.0), axis=1, keepdims=True).astype(jnp.int32)
 
+    landed(facts_core())
+    start(facts_z())
     others[1].wait()
     high = coarse[...].astype(BF16)
     halves[0:own_rows, :] = high
     halves[own_rows:, :] = (coarse[...] - high.astype(F32)).astype(BF16)
+    landed(facts_z())
 
     def choose(zt, carry):
-        for cc in range(CORES):
-            for xx in range(nx):
-                column = dof_column((y * CORES + cc) * subs + zt * nx + xx)
-                at = (cc * nx + xx) * ncl
-                select[at : at + ncl, :] = jnp.where(iota((ncl, order), 1) == column, 1.0, 0.0).astype(BF16)
-        both = lax.dot_general(select[...], halves[...], BY_ROWS, preferred_element_type=F32)
-        chosen[zt] = both[:, :own_rows] + both[:, own_rows:]
+        row = jnp.concatenate(
+            [facts_near[zt, cc, xx, 0:1, :ncl] for cc in range(CORES) for xx in range(nx)], axis=1
+        ).astype(jnp.int32)
+
+        def hot(part, carry):
+            at = pl.ds(pl.multiple_of(part * SH, SH), SH)
+            index = iota((SH, row.shape[1]), 0) + part * SH
+            select[at, :] = jnp.where(index == row, 1.0, 0.0).astype(BF16)
+            return carry
+
+        lax.fori_loop(0, order // SH, hot, 0)
+        both = jnp.dot(halves[...], select[...], preferred_element_type=F32)
+        chosen[zt] = both[:own_rows] + both[own_rows:]
         return carry
 
     lax.fori_loop(0, nz, choose, 0)
@@ -227,9 +277,18 @@
         start(columns_z())
         columns[c, x, lax.rem(z, half)] = chosen[z]
 
+    edge = basis_halo()
+    landed(edge)
+    extended[ncl : 2 * ncl, :SH] = jnp.where(lane_low, n_low * edge_in[0], 0.0)
+    extended[2 * ncl : 3 * ncl, tail0:] = jnp.where(lane_up, n_up * edge_in[1], 0.0)
+    low = extended[...] - extended[...].astype(BF16).astype(F32)
+    extended_t[:, :COLS] = extended[...].T.astype(BF16)
+    extended_t[:, COLS:] = low.T.astype(BF16)
+    sent(edge)
+    landed(far_y())
     for yy in range(ny):
         for zz in range(nz):
-            column = jnp.broadcast_to(dof_column((yy * CORES + c) * subs + zz * nx + x), (ncl, order))
+            column = jnp.broadcast_to(dof_column(facts_far[yy, zz, 0:1, :]), (ncl, order))
             at = (yy * nz + zz) * ncl
             pick_rows[at : at + ncl, :] = jnp.where(iota((ncl, order), 1) == column, 1.0, 0.0).astype(BF16)
 
@@ -239,7 +298,7 @@
 
         def turn_columns(tile, carry):
             at = pl.ds(pl.multiple_of(tile * SH, SH), SH)
-            swapped = lax.dot_general(matrix[at, tail0:], perm[...], BY_ROWS, preferred_element_type=F32)
+            swapped = jnp.dot(matrix[at, tail0:], perm_t[...], preferred_element_type=F32)
             matrix[at, tail0:] = swapped.astype(BF16)
             return carry
 
@@ -261,13 +320,8 @@
         sent(columns_z())
 
     sol[...] = jnp.zeros_like(sol)
-
-    def each_chunk(step):
-        def body(ch, carry):
-            step(ch)
-            return carry
-
-        lax.fori_loop(0, chunks, body, 0)
+    for copies in (facts_beside(), facts_x(), far_z(), facts_core(), far_y(), facts_z()):
+        sent(copies)
 
     def weigh(k, ch):
         landed(halo_local(ch))
@@ -305,32 +359,30 @@
     def sum_y(k, ch):
         copies = parts_y(k, ch)
         landed(copies)
-        total = part_y[ch, y]
+        whole = part_y[ch, y]
         for d in range(ny - 1):
-            total = total + got_y[k, ch, d]
-        part_z[ch] = total.reshape(nz, ncl, COLS)
-        start(parts_z(k, ch))
+            whole = whole + got_y[k, ch, d]
+        part_z[ch] = whole.reshape(nz, ncl, COLS)
+        got_z[k, ch, z] = part_z[ch, z]
+        start(parts_z(k, ch) + parts_beside(k, ch))
         sent(copies)
 
-    def sum_z(k, ch):
-        copies = parts_z(k, ch)
-        landed(copies)
-        total = part_z[ch, z]
-        for d in range(nz - 1):
-            total = total + got_z[k, ch, d]
-        picked[ch] = total
-        start(picked_halo(ch))
-        sent(copies)
+    def total(parts):
+        result = parts[0]
+        for i in range(1, nz):
+            result = result + parts[i]
+        return result
 
     def advance(k, ch):
-        near = picked_halo(ch)
-        landed(near)
+        parts = parts_z(k, ch) + parts_beside(k, ch)
+        landed(parts)
         halo = halo_field(ch)
         landed(halo)
         stacked = jnp.concatenate(
-            [picked[ch], picked_near[ch, 0], picked_near[ch, 1], jnp.zeros((COLS - 3 * ncl, COLS), F32)], axis=0
+            [total(got_z.at[k, ch]), total(near_z.at[k, ch, 0]), total(near_z.at[k, ch, 1]), jnp.zeros((COLS - 3 * ncl, COLS), F32)], axis=0
         ).astype(BF16)
-        sent(near)
+        stacked = jnp.concatenate([stacked, stacked], axis=0)
+        sent(parts)
         sent(halo)
         for tile in range(tiles):
             change = field[ch, rows(tile), :] + jnp.dot(
@@ -358,12 +410,6 @@
         landed(copies)
         start(columns_core())
         sent(copies)
-        edge = basis_halo()
-        landed(edge)
-        extended[ncl : 2 * ncl, :SH] = jnp.where(lane_low, n_low * edge_in[0], 0.0)
-        extended[2 * ncl : 3 * ncl, tail0:] = jnp.where(lane_up, n_up * edge_in[1], 0.0)
-        extended_t[...] = extended[...].T.astype(BF16)
-        sent(edge)
         landed(columns_core())
         wide = CORES * nx * ncl
         for cc in range(CORES):
@@ -372,32 +418,51 @@
                     block = columns[cc, xx, i]
                     high = block.astype(BF16)
                     at = ((cc * half + i) * nx + xx) * own_rows
-                    columns_hl[:wide, at : at + own_rows] = high
-                    columns_hl[wide:, at : at + own_rows] = (block - high.astype(F32)).astype(BF16)
+                    columns_hl[at : at + own_rows, :wide] = high
+                    columns_hl[at : at + own_rows, wide:] = (block - high.astype(F32)).astype(BF16)
+
+        step = min(SH, pick_rows.shape[0])
 
         def row_tile(tile, carry):
-            at = pl.ds(pl.multiple_of(tile * COLS, COLS), COLS)
-            both = lax.dot_general(pick_rows[at, :], columns_hl[...], BY_ROWS, preferred_element_type=F32)
+            at = pl.ds(pl.multiple_of(tile * step, step), step)
+            both = jnp.dot(pick_rows[at, :], columns_hl[...], preferred_element_type=F32)
             high = both[:, :wide].astype(BF16)
             coarse_k[at, :wide] = high
             coarse_k[at, wide : 2 * wide] = both[:, wide:].astype(BF16)
             coarse_k[at, 2 * wide :] = high
             return carry
 
-        lax.fori_loop(0, pick_rows.shape[0] // COLS, row_tile, 0)
+        lax.fori_loop(0, pick_rows.shape[0] // step, row_tile, 0)
         sent(columns_core())
 
-    def iteration(k, carry):
-        each_chunk(functools.partial(weigh, k))
-        each_chunk(functools.partial(to_core, k))
-        pl.when(k == 0)(finish_setup)
-        each_chunk(functools.partial(solve, k))
-        each_chunk(functools.partial(sum_y, k))
-        each_chunk(functools.partial(sum_z, k))
-        each_chunk(functools.partial(advance, k))
+    def each_chunk(step):
+        def body(ch, carry):
+            step(0, ch)
+            return carry
+
+        lax.fori_loop(0, chunks, body, 0)
+
+    lanes = chunks + 1
+
+    def tick(now, carry):
+        def run(step, late, first=0):
+            turn = now - late
+
+            @pl.when((turn >= first * lanes) & (turn < ITERS * lanes) & (lax.rem(turn + lanes, lanes) < chunks))
+            def _():
+                step(turn // lanes, lax.rem(turn, lanes))
+
+        run(to_core, 1, 1)
+        run(sum_y, 2)
+        run(solve, 1)
+        run(advance, 3)
+        run(weigh, 0, 1)
         return carry
 
-    lax.fori_loop(0, ITERS, iteration, 0)
+    each_chunk(weigh)
+    each_chunk(to_core)
+    finish_setup()
+    lax.fori_loop(1, ITERS * lanes + 3 - 1, tick, 0)
 
     out_copies = []
     for ch in range(chunks):
@@ -439,11 +504,6 @@
     ncl = coarse_basis.shape[2]
     own_rows, order = coarse_inverse.shape
     wide, tall = CORES * nx * ncl, ny * nz * ncl
-
-    mine = jnp.zeros((1, COLS), F32)
-    mine = mine.at[:, :ncl].set(coarse_dofs[0].astype(F32))
-    mine = mine.at[:, STIFF_LANE].set(stiffness[0])
-    info = lax.all_gather(mine, ("group", "sub"), axis=0, tiled=True)
 
     dma = pltpu.SemaphoreType.DMA
     vmem = pltpu.VMEM
@@ -466,28 +526,32 @@
         vmem((SH, COLS), F32),
         vmem((SH, COLS), F32),
         vmem((SH, SH), BF16),
+        vmem((SH, SH), BF16),
         vmem((2, ncl, SH), F32),
         vmem((2, ncl, SH), F32),
         vmem((COLS, unknowns), F32),
-        vmem((unknowns, COLS), BF16),
+        vmem((unknowns, 2 * COLS), BF16),
         vmem((tall, order), BF16),
-        vmem((wide, order), BF16),
-        vmem((nz, wide, own_rows), F32),
-        vmem((CORES, nx, half, wide, own_rows), F32),
-        vmem((2 * wide, order), BF16),
+        vmem((order, wide), BF16),
+        vmem((nz, own_rows, wide), F32),
+        vmem((CORES, nx, half, own_rows, wide), F32),
+        vmem((order, 2 * wide), BF16),
         vmem((tall, 3 * wide), BF16),
         vmem((ITERS, chunks, CORES, nx, ncl, COLS), F32),
         vmem((chunks, ny, nz * ncl, COLS), F32),
         vmem((ITERS, chunks, ny - 1, nz * ncl, COLS), F32),
         vmem((chunks, nz, ncl, COLS), F32),
-        vmem((ITERS, chunks, nz - 1, ncl, COLS), F32),
-        vmem((chunks, ncl, COLS), F32),
-        vmem((chunks, 2, ncl, COLS), F32),
+        vmem((ITERS, chunks, nz, ncl, COLS), F32),
+        vmem((ITERS, chunks, 2, nz, ncl, COLS), F32),
+        vmem((8, COLS), F32),
+        vmem((nz, CORES, nx, 8, COLS), F32),
+        vmem((ny, nz, 8, COLS), F32),
+        vmem((2, 8, COLS), F32),
         dma((chunks + 4,)),
         dma((2 * chunks,)),
         dma((chunks, 2)), dma((chunks, 2)),
         dma((chunks, 2)), dma((chunks, 2)),
-        dma((chunks, 2)), dma((chunks, 2)),
+        dma((chunks, 2, nz)), dma((ITERS, chunks, 2, nz)),
         dma((chunks, nx - 1)), dma((ITERS, chunks, nx - 1)),
         dma((chunks,)), dma((ITERS, chunks)),
         dma((chunks, ny - 1)), dma((ITERS, chunks, ny - 1)),
@@ -496,13 +560,21 @@
         dma((nx - 1,)), dma((nx - 1,)),
         dma((1,)), dma((1,)),
         dma((2,)), dma((2,)),
+        dma((nx - 1,)), dma((nx - 1,)),
+        dma((1,)), dma((1,)),
+        dma((nz - 1,)), dma((nz - 1,)),
+        dma((nz - 1,)), dma((nz - 1,)),
+        dma((ny - 1,)), dma((ny - 1,)),
+        dma((2,)), dma((2,)),
     ]
     anywhere = pl.BlockSpec(memory_space=pl.ANY)
     out = jax.ShapeDtypeStruct((unknowns, cases), F32)
     sol, res = pl.pallas_call(
         functools.partial(kernel, nx, nz, ny, chunks),
         out_shape=(out, out),
-        in_specs=[pl.BlockSpec(memory_space=pltpu.SMEM), pl.BlockSpec(memory_space=pltpu.VMEM)] + [anywhere] * 5,
+        in_specs=[pl.BlockSpec(memory_space=pltpu.SMEM)] * 2
+        + [pl.BlockSpec(memory_space=pltpu.VMEM)]
+        + [anywhere] * 5,
         out_specs=(anywhere, anywhere),
         scratch_shapes=scratch,
         compiler_params=pltpu.CompilerParams(
@@ -511,7 +583,8 @@
         cost_estimate=pl.CostEstimate(flops=2 * 9 * unknowns * unknowns * cases, bytes_accessed=1 << 24, transcendentals=0),
     )(
         shared_sizes[0, 0],
-        info,
+        stiffness[0],
+        coarse_dofs[0],
         load_cases[0, 0],
         schur_blocks[0, 0],
         neumann_inverse[0, 0],

time: 228 us -> 182 us (0.80)
  blocking collectives: 48.5 us -> 0 us
  Pallas kernels: 171 us -> 176 us
  other arithmetic: 2.58 us -> 0 us
    all_gather x1 -> x0, blocking collectives: 48.5 us -> none  [on_device(): info = lax.all_gather(mine, ('group', 'sub'), axis=0, tiled=True)]
    pallas_call x1, Pallas kernels: 171 us -> 176 us  [on_device(): pl.pallas_call(functools.partial(kernel, nx, nz, ny, chunks), out_shape=(...]
    another operation x3 -> x0, other arithmetic: 2.58 us -> none
where the time goes in v2:
time: 182 us; the launch traced here: 181 us
  Pallas kernels  176 us (97%)
  local copies, waits for them, and re-layouts  3.92 us (2%)
    pallas_call x1, Pallas kernels, on_device(): pl.pallas_call(functools.partial(kernel, nx, nz, ny, chunks), out_shape=(...  176 us
    unnamed x4, local copies, waits for them, and re-layouts  3.92 us

profile of v2, /device:TPU:0, one launch (start us, length us, event | category | flops | bytes accessed | tf_op | source)
XLA Modules:
  0.0 181.2 jit_solution(1210382523286706344)
XLA Ops:
  1.3 175.9 %shard_map.95 = (f32[1024,384]{1,0:T(8,128)}, f32[1024,384]{1,0:T(8,128)}) custom-call(s32[2]{0:T(128)} %bitcast.16, f32[1]{0:T(128)} %bitcast.9.stiff, s32[1,32]{1,0:T(1,128)} %bitcast.17, f32[1024,384]{1,0:T(8,128)} %bitcast.14, bf16[1024,1024]{1,0:T(8,128)(2,1)} %bitcast.12, bf16[1024,1024]{1,0:T(8,128)(2,1)} %bitcast.13, bf16[32,1024]{1,0:T(8,128)(2,1)} %bitcast.15, ...), custom_call_target="tpu_custom_call" | custom-call | flops 7247757312 | bytes 16777216 | tf_op jit(solution)/shard_map/pallas_call | solution.py:572
  177.2 0.0 copy-start
  177.2 2.8 %copy.13 = f32[1,1,1024,384]{3,2,1,0:T(8,128)} copy(f32[1,1,1024,384]{3,2,1,0:T(8,128)} %bitcast.11) | data formatting | bytes 3145728
  180.0 0.0 copy-done
  180.0 1.1 copy.14
Async XLA Ops:
  177.2 2.8 %copy-start = (f32[1024,384]{1,0:T(8,128)S(1)}, f32[1024,384]{1,0:T(8,128)}, u32[]{:S(2)}) copy-start(f32[1024,384]{1,0:T(8,128)} %get-tuple-element.5) | copy-start | bytes 4718596

commit v3 on v2

--- a/solution.py
+++ b/solution.py
@@ -30,7 +30,7 @@
     from_lower, from_upper, corr_lower, corr_upper,
     weight_head, weight_tail, perm, perm_t,
     edge_out, edge_in, extended, extended_t,
-    pick_rows, select, chosen, columns, columns_hl, coarse_k,
+    pick_rows, select, chosen, columns, columns_hl, coarse_k, coarse_part,
     terms, part_y, got_y, part_z, got_z, near_z,
     facts, facts_near, facts_far, facts_side,
     loc_sem, out_sem,
@@ -142,9 +142,9 @@
         own = columns.at[c, x]
         return [remote(own, own, gxs.at[d], gxr.at[d], to) for d, to in enumerate(x_peers)]
 
-    def columns_core():
-        own = columns.at[c]
-        return (remote(own, own, gcs.at[0], gcr.at[0], core_peer),)
+    def columns_core(j):
+        own = columns.at[c, lax.rem(x + nx - j, nx)]
+        return remote(own, own, gcs.at[j], gcr.at[j], core_peer)
 
     def facts_x():
         own = facts_near.at[z, c, x]
@@ -191,22 +191,33 @@
     peers = [*beside[0], *beside[1], *x_peers, *z_peers, *y_peers, core_peer]
     for peer in peers:
         pl.semaphore_signal(barrier, inc=1, device_id=peer, device_id_type=pl.DeviceIdType.MESH)
-    pl.semaphore_wait(barrier, len(peers))
-
-    start(facts_beside())
-    start(facts_x())
-    start(far_z())
 
     turn = lax.rem(share_up, SH)
     turn_back = lax.rem(2 * SH - share_up, SH)
+    moved = (iota((SH, SH), 0) + (SH - share_up)) & (SH - 1)
+    perm[...] = jnp.where(iota((SH, SH), 1) == moved, 1.0, 0.0).astype(BF16)
+    moved_lane = (iota((SH, SH), 1) + (SH - share_up)) & (SH - 1)
+    perm_t[...] = jnp.where(iota((SH, SH), 0) == moved_lane, 1.0, 0.0).astype(BF16)
     for ch in range(chunks):
         load_in[ch].wait()
         loads[ch, tail0:, :] = pltpu.roll(loads[ch, tail0:, :], turn, axis=0)
         local[ch, :, :] = loads[ch, :, :]
+    others[1].wait()
+    high = coarse[...].astype(BF16)
+    halves[0:own_rows, :] = high
+    halves[own_rows:, :] = (coarse[...] - high.astype(F32)).astype(BF16)
+
+    pl.semaphore_wait(barrier, len(peers))
+    start(facts_x())
+    start(facts_beside())
+    start(far_z())
+    for ch in range(chunks):
         start(halo_local(ch))
 
     landed(facts_x())
     start(facts_core())
+    landed(facts_core())
+    start(facts_z())
     landed(far_z())
     start(far_y())
     landed(facts_beside())
@@ -222,10 +233,6 @@
     weight_head[...] = jnp.where(in_low, w_low, 1.0)
     weight_tail[...] = jnp.where(in_up, w_up, 1.0)
 
-    moved = (iota((SH, SH), 0) + (SH - share_up)) & (SH - 1)
-    perm[...] = jnp.where(iota((SH, SH), 1) == moved, 1.0, 0.0).astype(BF16)
-    moved_lane = (iota((SH, SH), 1) + (SH - share_up)) & (SH - 1)
-    perm_t[...] = jnp.where(iota((SH, SH), 0) == moved_lane, 1.0, 0.0).astype(BF16)
     others[0].wait()
     basis_tail = jnp.dot(basis[:, tail0:], perm_t[...], preferred_element_type=F32)
     basis[:, tail0:] = basis_tail.astype(BF16)
@@ -244,15 +251,8 @@
         hit = iota((ncl, COLS), 0) == iota((ncl, COLS), 1)
         return jnp.sum(jnp.where(hit, row, 0.0), axis=1, keepdims=True).astype(jnp.int32)
 
-    landed(facts_core())
-    start(facts_z())
-    others[1].wait()
-    high = coarse[...].astype(BF16)
-    halves[0:own_rows, :] = high
-    halves[own_rows:, :] = (coarse[...] - high.astype(F32)).astype(BF16)
-    landed(facts_z())
-
-    def choose(zt, carry):
+
+    def choose(zt):
         row = jnp.concatenate(
             [facts_near[zt, cc, xx, 0:1, :ncl] for cc in range(CORES) for xx in range(nx)], axis=1
         ).astype(jnp.int32)
@@ -266,15 +266,16 @@
         lax.fori_loop(0, order // SH, hot, 0)
         both = jnp.dot(halves[...], select[...], preferred_element_type=F32)
         chosen[zt] = both[:own_rows] + both[own_rows:]
-        return carry
-
-    lax.fori_loop(0, nz, choose, 0)
 
     sends_here = z // half == c
+    choose(z)
+    landed(facts_z())
+    for d, copy in enumerate(columns_z()):
+        choose(lax.rem(z + d + 1, nz))
+        pl.when(sends_here)(copy.start)
 
     @pl.when(sends_here)
     def _():
-        start(columns_z())
         columns[c, x, lax.rem(z, half)] = chosen[z]
 
     edge = basis_halo()
@@ -311,6 +312,7 @@
         sender = lax.rem(z + nz - 1 - d, nz)
         pl.when(sender // half == c)(copy.wait_recv)
     start(columns_x())
+    columns_core(0).start()
 
     others[3].wait()
     align(schur)
@@ -332,6 +334,8 @@
         weighted[ch, tail0:, :] = (weight_tail[...] * tail).astype(BF16)
         terms[k, ch, c, x] = jnp.dot(basis[...], weighted[ch], preferred_element_type=F32)
         start(terms_x(k, ch))
+
+    def precondition(k, ch):
         for tile in edges + inner:
             product = jnp.dot(neumann[rows(tile), :], weighted[ch], preferred_element_type=F32)
             if tile == 0:
@@ -405,27 +409,28 @@
         sent(terms_x(k, ch))
         sent(terms_core(k, ch))
 
-    def finish_setup():
-        copies = columns_x()
-        landed(copies)
-        start(columns_core())
-        sent(copies)
-        landed(columns_core())
-        wide = CORES * nx * ncl
-        for cc in range(CORES):
-            for xx in range(nx):
-                for i in range(half):
-                    block = columns[cc, xx, i]
-                    high = block.astype(BF16)
-                    at = ((cc * half + i) * nx + xx) * own_rows
-                    columns_hl[at : at + own_rows, :wide] = high
-                    columns_hl[at : at + own_rows, wide:] = (block - high.astype(F32)).astype(BF16)
-
+    wide = CORES * nx * ncl
+    depth = nx * half * own_rows
+
+    def split_slot(cc, slot):
+        for i in range(half):
+            block = columns[cc, slot, i]
+            high = block.astype(BF16)
+            at = pl.ds(pl.multiple_of(((cc * half + i) * nx + slot) * own_rows, own_rows), own_rows)
+            columns_hl[at, :wide] = high
+            columns_hl[at, wide:] = (block - high.astype(F32)).astype(BF16)
+
+    def pick_half(cc, finish):
         step = min(SH, pick_rows.shape[0])
+        inside = pl.ds(pl.multiple_of(cc * depth, depth), depth)
 
         def row_tile(tile, carry):
             at = pl.ds(pl.multiple_of(tile * step, step), step)
-            both = jnp.dot(pick_rows[at, :], columns_hl[...], preferred_element_type=F32)
+            both = jnp.dot(pick_rows[at, inside], columns_hl[inside, :], preferred_element_type=F32)
+            if not finish:
+                coarse_part[at, :] = both
+                return carry
+            both = both + coarse_part[at, :]
             high = both[:, :wide].astype(BF16)
             coarse_k[at, :wide] = high
             coarse_k[at, wide : 2 * wide] = both[:, wide:].astype(BF16)
@@ -433,7 +438,21 @@
             return carry
 
         lax.fori_loop(0, pick_rows.shape[0] // step, row_tile, 0)
-        sent(columns_core())
+
+    def finish_setup():
+        to_peer = [columns_core(j) for j in range(nx)]
+        split_slot(c, x)
+        for d, copy in enumerate(columns_x()):
+            copy.wait_recv()
+            to_peer[d + 1].start()
+            split_slot(c, lax.rem(x + nx - d - 1, nx))
+        pick_half(c, False)
+        landed(to_peer)
+        for slot in range(nx):
+            split_slot(1 - c, slot)
+        pick_half(1 - c, True)
+        sent(columns_x())
+        sent(to_peer)
 
     def each_chunk(step):
         def body(ch, carry):
@@ -442,7 +461,7 @@
 
         lax.fori_loop(0, chunks, body, 0)
 
-    lanes = chunks + 1
+    lanes = chunks + 2
 
     def tick(now, carry):
         def run(step, late, first=0):
@@ -452,14 +471,16 @@
             def _():
                 step(turn // lanes, lax.rem(turn, lanes))
 
+        run(weigh, 0, 1)
         run(to_core, 1, 1)
         run(sum_y, 2)
         run(solve, 1)
+        run(precondition, 0, 1)
         run(advance, 3)
-        run(weigh, 0, 1)
         return carry
 
     each_chunk(weigh)
+    each_chunk(precondition)
     each_chunk(to_core)
     finish_setup()
     lax.fori_loop(1, ITERS * lanes + 3 - 1, tick, 0)
@@ -537,6 +558,7 @@
         vmem((CORES, nx, half, own_rows, wide), F32),
         vmem((order, 2 * wide), BF16),
         vmem((tall, 3 * wide), BF16),
+        vmem((tall, 2 * wide), F32),
         vmem((ITERS, chunks, CORES, nx, ncl, COLS), F32),
         vmem((chunks, ny, nz * ncl, COLS), F32),
         vmem((ITERS, chunks, ny - 1, nz * ncl, COLS), F32),
@@ -558,7 +580,7 @@
         dma((chunks, nz - 1)), dma((ITERS, chunks, nz - 1)),
         dma((nz - 1,)), dma((nz - 1,)),
         dma((nx - 1,)), dma((nx - 1,)),
-        dma((1,)), dma((1,)),
+        dma((nx,)), dma((nx,)),
         dma((2,)), dma((2,)),
         dma((nx - 1,)), dma((nx - 1,)),
         dma((1,)), dma((1,)),

time: 182 us -> 172 us (0.945)
  Pallas kernels: 176 us -> 165 us
    pallas_call x1, Pallas kernels: 176 us -> 165 us  [on_device(): pl.pallas_call(functools.partial(kernel, nx, nz, ny, chunks), out_shape=(...]
where the time goes in v3:
time: 172 us; the launch traced here: 170 us
  Pallas kernels  165 us (96%)
  local copies, waits for them, and re-layouts  3.92 us (2%)
    pallas_call x1, Pallas kernels, on_device(): pl.pallas_call(functools.partial(kernel, nx, nz, ny, chunks), out_shape=(...  165 us
    unnamed x4, local copies, waits for them, and re-layouts  3.92 us

profile of v3, /device:TPU:0, one launch (start us, length us, event | category | flops | bytes accessed | tf_op | source)
XLA Modules:
  0.0 170.3 jit_solution(4149336074425224773)
XLA Ops:
  1.3 165.1 %shard_map.95 = (f32[1024,384]{1,0:T(8,128)}, f32[1024,384]{1,0:T(8,128)}) custom-call(s32[2]{0:T(128)} %bitcast.16, f32[1]{0:T(128)} %bitcast.9.stiff, s32[1,32]{1,0:T(1,128)} %bitcast.17, f32[1024,384]{1,0:T(8,128)} %bitcast.14, bf16[1024,1024]{1,0:T(8,128)(2,1)} %bitcast.12, bf16[1024,1024]{1,0:T(8,128)(2,1)} %bitcast.13, bf16[32,1024]{1,0:T(8,128)(2,1)} %bitcast.15, ...), custom_call_target="tpu_custom_call" | custom-call | flops 7247757312 | bytes 16777216 | tf_op jit(solution)/shard_map/pallas_call | solution.py:594
  166.4 0.0 copy-start
  166.4 2.8 %copy.13 = f32[1,1,1024,384]{3,2,1,0:T(8,128)} copy(f32[1,1,1024,384]{3,2,1,0:T(8,128)} %bitcast.11) | data formatting | bytes 3145728
  169.1 0.0 copy-done
  169.1 1.1 copy.14
Async XLA Ops:
  166.4 2.8 %copy-start = (f32[1024,384]{1,0:T(8,128)S(1)}, f32[1024,384]{1,0:T(8,128)}, u32[]{:S(2)}) copy-start(f32[1024,384]{1,0:T(8,128)} %get-tuple-element.5) | copy-start | bytes 4718596

commit v4 on v3

--- a/solution.py
+++ b/solution.py
@@ -138,9 +138,9 @@
             for d, to in enumerate(z_peers)
         ]
 
-    def columns_x():
-        own = columns.at[c, x]
-        return [remote(own, own, gxs.at[d], gxr.at[d], to) for d, to in enumerate(x_peers)]
+    def columns_x(i):
+        own = columns.at[c, x, i]
+        return [remote(own, own, gxs.at[d, i], gxr.at[d, i], to) for d, to in enumerate(x_peers)]
 
     def columns_core(j):
         own = columns.at[c, lax.rem(x + nx - j, nx)]
@@ -269,14 +269,16 @@
 
     sends_here = z // half == c
     choose(z)
+
+    @pl.when(sends_here)
+    def _():
+        columns[c, x, lax.rem(z, half)] = chosen[z]
+        start(columns_x(lax.rem(z, half)))
+
     landed(facts_z())
     for d, copy in enumerate(columns_z()):
         choose(lax.rem(z + d + 1, nz))
         pl.when(sends_here)(copy.start)
-
-    @pl.when(sends_here)
-    def _():
-        columns[c, x, lax.rem(z, half)] = chosen[z]
 
     edge = basis_halo()
     landed(edge)
@@ -311,7 +313,8 @@
     for d, copy in enumerate(columns_z()):
         sender = lax.rem(z + nz - 1 - d, nz)
         pl.when(sender // half == c)(copy.wait_recv)
-    start(columns_x())
+    for i in range(half):
+        pl.when(c * half + i != z)(functools.partial(lambda i: start(columns_x(i)), i))
     columns_core(0).start()
 
     others[3].wait()
@@ -442,8 +445,9 @@
     def finish_setup():
         to_peer = [columns_core(j) for j in range(nx)]
         split_slot(c, x)
-        for d, copy in enumerate(columns_x()):
-            copy.wait_recv()
+        pieces = [columns_x(i) for i in range(half)]
+        for d in range(nx - 1):
+            landed([piece[d] for piece in pieces])
             to_peer[d + 1].start()
             split_slot(c, lax.rem(x + nx - d - 1, nx))
         pick_half(c, False)
@@ -451,7 +455,8 @@
         for slot in range(nx):
             split_slot(1 - c, slot)
         pick_half(1 - c, True)
-        sent(columns_x())
+        for piece in pieces:
+            sent(piece)
         sent(to_peer)
 
     def each_chunk(step):
@@ -579,7 +584,7 @@
         dma((chunks, ny - 1)), dma((ITERS, chunks, ny - 1)),
         dma((chunks, nz - 1)), dma((ITERS, chunks, nz - 1)),
         dma((nz - 1,)), dma((nz - 1,)),
-        dma((nx - 1,)), dma((nx - 1,)),
+        dma((nx - 1, half)), dma((nx - 1, half)),
         dma((nx,)), dma((nx,)),
         dma((2,)), dma((2,)),
         dma((nx - 1,)), dma((nx - 1,)),

time: 172 us -> 171 us (level)
  no operation moved by 1% of the time
where the time goes in v4:
time: 171 us
  Pallas kernels  165 us (96%)
  local copies, waits for them, and re-layouts  3.92 us (2%)
    pallas_call x1, Pallas kernels, on_device(): pl.pallas_call(functools.partial(kernel, nx, nz, ny, chunks), out_shape=(...  165 us
    unnamed x4, local copies, waits for them, and re-layouts  3.92 us

profile of v4, /device:TPU:0, one launch (start us, length us, event | category | flops | bytes accessed | tf_op | source)
XLA Modules:
  0.0 170.6 jit_solution(8470769167386071835)
XLA Ops:
  1.3 165.4 %shard_map.95 = (f32[1024,384]{1,0:T(8,128)}, f32[1024,384]{1,0:T(8,128)}) custom-call(s32[2]{0:T(128)} %bitcast.16, f32[1]{0:T(128)} %bitcast.9.stiff, s32[1,32]{1,0:T(1,128)} %bitcast.17, f32[1024,384]{1,0:T(8,128)} %bitcast.14, bf16[1024,1024]{1,0:T(8,128)(2,1)} %bitcast.12, bf16[1024,1024]{1,0:T(8,128)(2,1)} %bitcast.13, bf16[32,1024]{1,0:T(8,128)(2,1)} %bitcast.15, ...), custom_call_target="tpu_custom_call" | custom-call | flops 7247757312 | bytes 16777216 | tf_op jit(solution)/shard_map/pallas_call | solution.py:599
  166.7 0.0 copy-start
  166.7 2.8 %copy.13 = f32[1,1,1024,384]{3,2,1,0:T(8,128)} copy(f32[1,1,1024,384]{3,2,1,0:T(8,128)} %bitcast.11) | data formatting | bytes 3145728
  169.5 0.0 copy-done
  169.5 1.1 copy.14
Async XLA Ops:
  166.7 2.8 %copy-start = (f32[1024,384]{1,0:T(8,128)S(1)}, f32[1024,384]{1,0:T(8,128)}, u32[]{:S(2)}) copy-start(f32[1024,384]{1,0:T(8,128)} %get-tuple-element.5) | copy-start | bytes 4718596

commit v5 on v4

--- a/solution.py
+++ b/solution.py
@@ -358,8 +358,10 @@
         mine = terms[k, ch].reshape(CORES * nx * ncl, COLS)
         high = mine.astype(BF16)
         low = (mine - high.astype(F32)).astype(BF16)
-        stacked = jnp.concatenate([high, high, low], axis=0)
-        solved = jnp.dot(coarse_k[...], stacked, preferred_element_type=F32)
+        both = jnp.concatenate([high, low], axis=1)
+        pair = jnp.dot(coarse_k[:, :wide], both, preferred_element_type=F32)
+        rest = jnp.dot(coarse_k[:, wide:], high, preferred_element_type=F32)
+        solved = pair[:, :COLS] + (pair[:, COLS:] + rest)
         part_y[ch] = solved.reshape(ny, nz * ncl, COLS)
         start(parts_y(k, ch))
 
@@ -434,10 +436,8 @@
                 coarse_part[at, :] = both
                 return carry
             both = both + coarse_part[at, :]
-            high = both[:, :wide].astype(BF16)
-            coarse_k[at, :wide] = high
-            coarse_k[at, wide : 2 * wide] = both[:, wide:].astype(BF16)
-            coarse_k[at, 2 * wide :] = high
+            coarse_k[at, :wide] = both[:, :wide].astype(BF16)
+            coarse_k[at, wide:] = both[:, wide:].astype(BF16)
             return carry
 
         lax.fori_loop(0, pick_rows.shape[0] // step, row_tile, 0)
@@ -562,7 +562,7 @@
         vmem((nz, own_rows, wide), F32),
         vmem((CORES, nx, half, own_rows, wide), F32),
         vmem((order, 2 * wide), BF16),
-        vmem((tall, 3 * wide), BF16),
+        vmem((tall, 2 * wide), BF16),
         vmem((tall, 2 * wide), F32),
         vmem((ITERS, chunks, CORES, nx, ncl, COLS), F32),
         vmem((chunks, ny, nz * ncl, COLS), F32),

time: 171 us -> 171 us (level)
  no operation moved by 1% of the time
where the time goes in v5:
time: 171 us
  Pallas kernels  165 us (96%)
  local copies, waits for them, and re-layouts  3.92 us (2%)
    pallas_call x1, Pallas kernels, on_device(): pl.pallas_call(functools.partial(kernel, nx, nz, ny, chunks), out_shape=(...  165 us
    unnamed x4, local copies, waits for them, and re-layouts  3.92 us

profile of v5, /device:TPU:0, one launch (start us, length us, event | category | flops | bytes accessed | tf_op | source)
XLA Modules:
  0.0 170.7 jit_solution(9110272914846823589)
XLA Ops:
  1.3 165.5 %shard_map.95 = (f32[1024,384]{1,0:T(8,128)}, f32[1024,384]{1,0:T(8,128)}) custom-call(s32[2]{0:T(128)} %bitcast.16, f32[1]{0:T(128)} %bitcast.9.stiff, s32[1,32]{1,0:T(1,128)} %bitcast.17, f32[1024,384]{1,0:T(8,128)} %bitcast.14, bf16[1024,1024]{1,0:T(8,128)(2,1)} %bitcast.12, bf16[1024,1024]{1,0:T(8,128)(2,1)} %bitcast.13, bf16[32,1024]{1,0:T(8,128)(2,1)} %bitcast.15, ...), custom_call_target="tpu_custom_call" | custom-call | flops 7247757312 | bytes 16777216 | tf_op jit(solution)/shard_map/pallas_call | solution.py:599
  166.8 0.0 copy-start
  166.8 2.8 %copy.13 = f32[1,1,1024,384]{3,2,1,0:T(8,128)} copy(f32[1,1,1024,384]{3,2,1,0:T(8,128)} %bitcast.11) | data formatting | bytes 3145728
  169.5 0.0 copy-done
  169.6 1.1 copy.14
Async XLA Ops:
  166.8 2.8 %copy-start = (f32[1024,384]{1,0:T(8,128)S(1)}, f32[1024,384]{1,0:T(8,128)}, u32[]{:S(2)}) copy-start(f32[1024,384]{1,0:T(8,128)} %get-tuple-element.5) | copy-start | bytes 4718596
